TPU v7x, 32 devices: a whole 2x2x4 slice. The times are simulated.
32 devices in a mesh: bx: 8 (over z, x), by: 4 (over y, core).
Axes of the slice: x: 2, y: 2, z: 4, core: 2. Of those that a mesh axis runs over, the one named last changes fastest.
Arguments:
- positions: float32 [4096, 3, 256], P(('bx', 'by')), may hold values from 0 to 4, as said below
- strengths: float32 [4096, 3, 256], P(('bx', 'by')), may hold values from -0.4 to 0.4
- blob_count: int32 [4096], P(('bx', 'by')), may hold values from 64 to 256
- split_counts: int32 [32, 32], P(('bx', 'by')), may hold values from 0 to 4, as said below
- ghost_ids: int32 [32, 8, 16], P(('bx', 'by')), may hold values from 0 to 63, as said below
- near_list: int32 [2048, 8], P(('bx', 'by')), may hold values from 0 to 191, as said below
Outputs:
- owned_blobs: float32 [2048, 6, 256], P(('bx', 'by'))
- velocity: float32 [2048, 3, 256], P(('bx', 'by'))
Inputs may be any that keep to these rules, and one draw needn't show every extreme that they name: Each sender's leaves occupy its first slots, grouped by receiver in increasing order, split_counts[s, d] of them for receiver d. Every column of split_counts sums to exactly 64, and every column has an entry equal to 4. `positions`: the blobs of each used slot lie in the box of the leaf that the slot becomes; leaves are boxes of side 0.25 on a grid, and each device's leaves fill a 2 x 2 x 16 block of that grid placed by its bx and by indices. `ghost_ids`: the leaves named for a direction lie on the neighbour's face toward the reader. `near_list`: entry 0 of a leaf's list is the leaf itself; the others are leaves near it. An index 64 + q * 16 + g names ghost g of neighbour direction q and appears only where that neighbouring device exists.
All inputs are finite; a program needn't handle non-finite values.
Results may differ from a plain program's by a relative error of at most 0.0003.
Values sent between devices are 32-bit elements; how exact they have to be, the bound alone decides.
A program may use at most 64 MiB of HBM per device.

v0:
```python
import math

import jax
import jax.numpy as jnp
from jax import lax
from jax.sharding import PartitionSpec as P

CORE_SQUARED = 0.01
OFFSET_ROWS = (-1, -1, -1, 0, 0, 1, 1, 1)
OFFSET_COLS = (-1, 0, 1, -1, 1, -1, 0, 1)


def shifted(shard, axis, by):
    devices = lax.axis_size(axis)
    pairs = [(i, i + by) for i in range(devices) if 0 <= i + by < devices]
    return lax.ppermute(shard, axis, pairs)


def induced(targets, sources):
    delta_x = targets[:, 0, :, None] - sources[:, 0, None, :]
    delta_y = targets[:, 1, :, None] - sources[:, 1, None, :]
    delta_z = targets[:, 2, :, None] - sources[:, 2, None, :]
    inverse = lax.rsqrt(delta_x * delta_x + delta_y * delta_y + delta_z * delta_z + CORE_SQUARED)
    inverse_cube = inverse * inverse * inverse
    alpha_x = sources[:, 3, None, :]
    alpha_y = sources[:, 4, None, :]
    alpha_z = sources[:, 5, None, :]
    speed_x = jnp.sum((alpha_y * delta_z - alpha_z * delta_y) * inverse_cube, axis=2)
    speed_y = jnp.sum((alpha_z * delta_x - alpha_x * delta_z) * inverse_cube, axis=2)
    speed_z = jnp.sum((alpha_x * delta_y - alpha_y * delta_x) * inverse_cube, axis=2)
    return jnp.stack([speed_x, speed_y, speed_z], axis=1) / (4.0 * math.pi)


def request_move(values, off_a, off_b):
    if off_a != 0:
        values = shifted(values, "bx", off_a)
    if off_b != 0:
        values = shifted(values, "by", off_b)
    return values


def reply_move(values, off_a, off_b):
    if off_a != 0:
        values = shifted(values, "bx", off_a)
    if off_b != 0:
        values = shifted(values, "by", off_b)
    return values


def local(positions, strengths, blob_count, split_counts, ghost_ids, near_list):
    rows_bx = lax.axis_size("bx")
    rows_by = lax.axis_size("by")
    devices = rows_bx * rows_by
    slots = positions.shape[0]
    pair_most = slots // devices
    leaf = positions.shape[2]
    own = near_list.shape[0]
    counts_row = split_counts[0]
    starts = jnp.cumsum(counts_row) - counts_row
    within = jnp.arange(pair_most, dtype=jnp.int32)
    pick = jnp.minimum(starts[:, None] + within[None, :], slots - 1).reshape(-1)
    valid = (within[None, :] < counts_row[:, None]).reshape(-1)
    stacked = jnp.concatenate([positions, strengths], axis=1)[pick]
    sent_count = jnp.where(valid, blob_count[pick], 0)
    sent_live = (jnp.arange(leaf, dtype=jnp.int32)[None, :] < sent_count[:, None]).astype(
        jnp.float32
    )
    outgoing = (stacked * sent_live[:, None, :]).reshape(devices, pair_most, 6, leaf)
    out_count = sent_count.astype(jnp.float32).reshape(devices, pair_most)
    arrived, arrived_count = (
        lax.all_to_all(outgoing, ("bx", "by"), split_axis=0, concat_axis=0, tiled=True),
        lax.all_to_all(out_count, ("bx", "by"), split_axis=0, concat_axis=0, tiled=True),
    )
    arrived_valid = arrived_count > 0.0
    per_source = jnp.sum(arrived_valid.astype(jnp.int32), axis=1)
    prefix = jnp.cumsum(per_source) - per_source
    placed = jnp.where(arrived_valid, prefix[:, None] + within[None, :], own).reshape(-1)
    selector = (jnp.arange(own, dtype=jnp.int32)[:, None] == placed[None, :]).astype(jnp.float32)
    owned_blobs = jnp.dot(
        selector, arrived.reshape(devices * pair_most, 6 * leaf), precision=lax.Precision.HIGHEST
    ).reshape(own, 6, leaf)
    own_count = jnp.dot(selector, arrived_count.reshape(-1), precision=lax.Precision.HIGHEST)
    own_live = (jnp.arange(leaf, dtype=jnp.float32)[None, :] < own_count[:, None]).astype(
        jnp.float32
    )
    ghost_blocks = []
    for direction in range(8):
        off_a = OFFSET_ROWS[direction]
        off_b = OFFSET_COLS[direction]
        request = request_move(ghost_ids[0, direction], off_a, off_b)
        served = owned_blobs[request]
        ghost_blocks.append(reply_move(served, -off_a, -off_b))
    combined = jnp.concatenate([owned_blobs] + ghost_blocks, axis=0)
    near_count = near_list.shape[1]
    turns = 16
    block_leaves = own // turns

    def one_block(block_index):
        first_row = block_index * block_leaves
        targets = lax.dynamic_slice_in_dim(owned_blobs, first_row, block_leaves, 0)
        near_rows = lax.dynamic_slice_in_dim(near_list, first_row, block_leaves, 0)
        live_block = lax.dynamic_slice_in_dim(own_live, first_row, block_leaves, 0)

        def add_neighbour(index, total):
            column = lax.dynamic_slice_in_dim(near_rows, index, 1, 1)[:, 0]
            sources = combined[column]
            return total + induced(targets, sources)

        start_total = jnp.zeros((block_leaves, 3, leaf), jnp.float32)
        summed = lax.fori_loop(0, near_count, add_neighbour, start_total)
        return summed * live_block[:, None, :]

    velocity = lax.map(one_block, jnp.arange(turns, dtype=jnp.int32)).reshape(own, 3, leaf)
    return (owned_blobs, velocity)


def solution(mesh):
    placed = (
        P(("bx", "by"), None, None),
        P(("bx", "by"), None, None),
        P(("bx", "by")),
        P(("bx", "by"), None),
        P(("bx", "by"), None, None),
        P(("bx", "by"), None),
    )
    return jax.shard_map(
        local,
        mesh=mesh,
        in_specs=placed,
        out_specs=(P(("bx", "by"), None, None), P(("bx", "by"), None, None)),
        check_vma=False,
    )
```

profile of v0, /device:TPU:11, one launch (start us, length us, event | category | flops | bytes accessed | tf_op | source)
XLA Modules:
  0.0 437.9 jit_solution(17731735003689501599)
XLA Ops:
  5.3 6.3 %all-to-all-start = ((f32[32,1,4]{2,1,0:T(1,128)}), f32[32,1,4]{2,1,0:T(1,128)S(1)}, u32[]{:S(2)}, u32[]{:S(2)}) async-start(f32[32,1,4]{2,1,0:T(1,128)} %copy.93), calls=%async_computation | async-start | bytes 32768 | tf_op jit(solution)/shard_map/all_to_all | solution.py:72
  12.6 2.2 collective-permute-start
  14.8 3.1 collective-permute-start.4
  17.9 2.0 collective-permute-start.6
  19.9 3.0 collective-permute-start.10
  22.9 4.3 collective-permute-start.14
  31.0 3.3 collective-permute-start.12
  34.3 2.2 collective-permute-start.20
  36.5 4.0 collective-permute-start.18
  40.5 1.9 collective-permute-start.1
  42.5 3.6 collective-permute-start.7
  46.1 1.9 collective-permute-start.15
  48.1 3.6 collective-permute-start.21
  51.8 2.8 all-to-all-start.1
  57.3 15.8 %all-to-all-done.1 = f32[32,4,6,256]{3,1,2,0:T(4,128)S(1)} async-done(((f32[32,4,6,256]{3,1,2,0:T(4,128)}), f32[32,4,6,256]{3,1,2,0:T(4,128)S(1)}, u32[]{:S(2)}, u32[]{:S(2)}) %all-to-all-start.1) | async-done | bytes 786464 | tf_op jit(solution)/shard_map/all_to_all | solution.py:71
  75.3 4.1 collective-permute-start.2
  79.5 2.3 collective-permute-done.2
  81.8 3.8 collective-permute-start.3
  86.3 3.9 collective-permute-start.5
  90.9 1.9 collective-permute-start.8
  93.4 2.2 collective-permute-start.11
  96.2 2.1 collective-permute-start.13
  100.2 3.4 collective-permute-start.16
  104.6 3.0 collective-permute-start.22
  107.6 1.9 collective-permute-start.9
  109.6 4.1 collective-permute-start.19
  113.6 4.5 %collective-permute-start.17 = (f32[16,6,256]{2,0,1:T(8,128)S(1)}, f32[16,6,256]{2,0,1:T(8,128)S(1)}, u32[]{:S(2)}, u32[]{:S(2)}) collective-permute-start(f32[16,6,256]{2,0,1:T(8,128)S(1)} %collective-permute-done.16), channel_id=1, source_target_pairs={{0,1},{1,2},{2,3},{4,5},{5,6},{6,7},{8,9},{9,10},{10,11},{12,13},{... | collective-permute-start | bytes 294920 | tf_op jit(solution)/shard_map/ppermute | solution.py:16
  118.1 1.9 collective-permute-start.23
  120.2 3.9 collective-permute-done.23
  124.8 312.2 %while.25 = (s32[]{:T(128)}, f32[16,4,3,256]{3,1,0,2:T(4,128)S(1)}, s32[16]{0:T(128)S(1)}, s32[64,8]{0,1:T(8,128)S(1)}, f32[64,6,256]{2,0,1:T(8,128)S(1)}, /*ind...) while((s32[]{:T(128)}, f32[16,4,3,256]{3,1,0,2:T(4,128)S(1)}, ...), condition=%wide.region_9.10_spmd, body=%wide.region_3.9_spmd.sunk | while | flops 6832149 | bytes 348834 | solution.py:113
  126.2 18.1 %while.26 = (s32[]{:T(128)}, f32[4,3,256]{2,0,1:T(4,128)S(1)}, s32[4,8]{0,1:T(8,128)S(1)}, f32[192,6,256]{2,1,0:T(8,128)S(1)}, f32[4,6,256]{2,0,1:T(4,128)S(1)}, /*index=5*/s32[]{:T(128)}, s32[]{:T(128)}) while((s32[]{:T(128)}, f32[4,3,256]{2,0,1:T(4,128)S(1)}, s32[4,8]{0,1:T(8,128)S(1)}, f32[192,6,256]{2,1,0:T(8,128)S(1)}, ...), condition=%wide.region_8.8_spmd.clone, body=%wide.region_4.7_spmd.clone.sunk | while | flops 6829071 | bytes 262299 | solution.py:110
  133.7 1.6 fusion.34
  135.9 1.6 fusion.34
  138.2 1.6 fusion.34
  140.5 1.6 fusion.34
  142.7 1.6 fusion.34
  145.7 18.1 %while.26 = (s32[]{:T(128)}, f32[4,3,256]{2,0,1:T(4,128)S(1)}, s32[4,8]{0,1:T(8,128)S(1)}, f32[192,6,256]{2,1,0:T(8,128)S(1)}, f32[4,6,256]{2,0,1:T(4,128)S(1)}, /*index=5*/s32[]{:T(128)}, s32[]{:T(128)}) while((s32[]{:T(128)}, f32[4,3,256]{2,0,1:T(4,128)S(1)}, s32[4,8]{0,1:T(8,128)S(1)}, f32[192,6,256]{2,1,0:T(8,128)S(1)}, ...), condition=%wide.region_8.8_spmd.clone, body=%wide.region_4.7_spmd.clone.sunk | while | flops 6829071 | bytes 262299 | solution.py:110
  146.4 1.6 fusion.34
  148.6 1.6 fusion.34
  150.9 1.6 fusion.34
  153.2 1.6 fusion.34
  155.4 1.6 fusion.34
  157.7 1.6 fusion.34
  160.0 1.6 fusion.34
  165.2 18.1 %while.26 = (s32[]{:T(128)}, f32[4,3,256]{2,0,1:T(4,128)S(1)}, s32[4,8]{0,1:T(8,128)S(1)}, f32[192,6,256]{2,1,0:T(8,128)S(1)}, f32[4,6,256]{2,0,1:T(4,128)S(1)}, /*index=5*/s32[]{:T(128)}, s32[]{:T(128)}) while((s32[]{:T(128)}, f32[4,3,256]{2,0,1:T(4,128)S(1)}, s32[4,8]{0,1:T(8,128)S(1)}, f32[192,6,256]{2,1,0:T(8,128)S(1)}, ...), condition=%wide.region_8.8_spmd.clone, body=%wide.region_4.7_spmd.clone.sunk | while | flops 6829071 | bytes 262299 | solution.py:110
  165.9 1.6 fusion.34
  168.1 1.6 fusion.34
  170.4 1.6 fusion.34
  172.7 1.6 fusion.34
  174.9 1.6 fusion.34
  181.7 1.6 fusion.34
  184.7 18.1 %while.26 = (s32[]{:T(128)}, f32[4,3,256]{2,0,1:T(4,128)S(1)}, s32[4,8]{0,1:T(8,128)S(1)}, f32[192,6,256]{2,1,0:T(8,128)S(1)}, f32[4,6,256]{2,0,1:T(4,128)S(1)}, /*index=5*/s32[]{:T(128)}, s32[]{:T(128)}) while((s32[]{:T(128)}, f32[4,3,256]{2,0,1:T(4,128)S(1)}, s32[4,8]{0,1:T(8,128)S(1)}, f32[192,6,256]{2,1,0:T(8,128)S(1)}, ...), condition=%wide.region_8.8_spmd.clone, body=%wide.region_4.7_spmd.clone.sunk | while | flops 6829071 | bytes 262299 | solution.py:110
  204.2 18.1 %while.26 = (s32[]{:T(128)}, f32[4,3,256]{2,0,1:T(4,128)S(1)}, s32[4,8]{0,1:T(8,128)S(1)}, f32[192,6,256]{2,1,0:T(8,128)S(1)}, f32[4,6,256]{2,0,1:T(4,128)S(1)}, /*index=5*/s32[]{:T(128)}, s32[]{:T(128)}) while((s32[]{:T(128)}, f32[4,3,256]{2,0,1:T(4,128)S(1)}, s32[4,8]{0,1:T(8,128)S(1)}, f32[192,6,256]{2,1,0:T(8,128)S(1)}, ...), condition=%wide.region_8.8_spmd.clone, body=%wide.region_4.7_spmd.clone.sunk | while | flops 6829071 | bytes 262299 | solution.py:110
  223.8 18.1 %while.26 = (s32[]{:T(128)}, f32[4,3,256]{2,0,1:T(4,128)S(1)}, s32[4,8]{0,1:T(8,128)S(1)}, f32[192,6,256]{2,1,0:T(8,128)S(1)}, f32[4,6,256]{2,0,1:T(4,128)S(1)}, /*index=5*/s32[]{:T(128)}, s32[]{:T(128)}) while((s32[]{:T(128)}, f32[4,3,256]{2,0,1:T(4,128)S(1)}, s32[4,8]{0,1:T(8,128)S(1)}, f32[192,6,256]{2,1,0:T(8,128)S(1)}, ...), condition=%wide.region_8.8_spmd.clone, body=%wide.region_4.7_spmd.clone.sunk | while | flops 6829071 | bytes 262299 | solution.py:110
  243.3 18.1 %while.26 = (s32[]{:T(128)}, f32[4,3,256]{2,0,1:T(4,128)S(1)}, s32[4,8]{0,1:T(8,128)S(1)}, f32[192,6,256]{2,1,0:T(8,128)S(1)}, f32[4,6,256]{2,0,1:T(4,128)S(1)}, /*index=5*/s32[]{:T(128)}, s32[]{:T(128)}) while((s32[]{:T(128)}, f32[4,3,256]{2,0,1:T(4,128)S(1)}, s32[4,8]{0,1:T(8,128)S(1)}, f32[192,6,256]{2,1,0:T(8,128)S(1)}, ...), condition=%wide.region_8.8_spmd.clone, body=%wide.region_4.7_spmd.clone.sunk | while | flops 6829071 | bytes 262299 | solution.py:110
  262.8 18.1 %while.26 = (s32[]{:T(128)}, f32[4,3,256]{2,0,1:T(4,128)S(1)}, s32[4,8]{0,1:T(8,128)S(1)}, f32[192,6,256]{2,1,0:T(8,128)S(1)}, f32[4,6,256]{2,0,1:T(4,128)S(1)}, /*index=5*/s32[]{:T(128)}, s32[]{:T(128)}) while((s32[]{:T(128)}, f32[4,3,256]{2,0,1:T(4,128)S(1)}, s32[4,8]{0,1:T(8,128)S(1)}, f32[192,6,256]{2,1,0:T(8,128)S(1)}, ...), condition=%wide.region_8.8_spmd.clone, body=%wide.region_4.7_spmd.clone.sunk | while | flops 6829071 | bytes 262299 | solution.py:110
  282.3 18.1 %while.26 = (s32[]{:T(128)}, f32[4,3,256]{2,0,1:T(4,128)S(1)}, s32[4,8]{0,1:T(8,128)S(1)}, f32[192,6,256]{2,1,0:T(8,128)S(1)}, f32[4,6,256]{2,0,1:T(4,128)S(1)}, /*index=5*/s32[]{:T(128)}, s32[]{:T(128)}) while((s32[]{:T(128)}, f32[4,3,256]{2,0,1:T(4,128)S(1)}, s32[4,8]{0,1:T(8,128)S(1)}, f32[192,6,256]{2,1,0:T(8,128)S(1)}, ...), condition=%wide.region_8.8_spmd.clone, body=%wide.region_4.7_spmd.clone.sunk | while | flops 6829071 | bytes 262299 | solution.py:110
  301.8 18.1 %while.26 = (s32[]{:T(128)}, f32[4,3,256]{2,0,1:T(4,128)S(1)}, s32[4,8]{0,1:T(8,128)S(1)}, f32[192,6,256]{2,1,0:T(8,128)S(1)}, f32[4,6,256]{2,0,1:T(4,128)S(1)}, /*index=5*/s32[]{:T(128)}, s32[]{:T(128)}) while((s32[]{:T(128)}, f32[4,3,256]{2,0,1:T(4,128)S(1)}, s32[4,8]{0,1:T(8,128)S(1)}, f32[192,6,256]{2,1,0:T(8,128)S(1)}, ...), condition=%wide.region_8.8_spmd.clone, body=%wide.region_4.7_spmd.clone.sunk | while | flops 6829071 | bytes 262299 | solution.py:110
  321.3 18.1 %while.26 = (s32[]{:T(128)}, f32[4,3,256]{2,0,1:T(4,128)S(1)}, s32[4,8]{0,1:T(8,128)S(1)}, f32[192,6,256]{2,1,0:T(8,128)S(1)}, f32[4,6,256]{2,0,1:T(4,128)S(1)}, /*index=5*/s32[]{:T(128)}, s32[]{:T(128)}) while((s32[]{:T(128)}, f32[4,3,256]{2,0,1:T(4,128)S(1)}, s32[4,8]{0,1:T(8,128)S(1)}, f32[192,6,256]{2,1,0:T(8,128)S(1)}, ...), condition=%wide.region_8.8_spmd.clone, body=%wide.region_4.7_spmd.clone.sunk | while | flops 6829071 | bytes 262299 | solution.py:110
  340.8 18.1 %while.26 = (s32[]{:T(128)}, f32[4,3,256]{2,0,1:T(4,128)S(1)}, s32[4,8]{0,1:T(8,128)S(1)}, f32[192,6,256]{2,1,0:T(8,128)S(1)}, f32[4,6,256]{2,0,1:T(4,128)S(1)}, /*index=5*/s32[]{:T(128)}, s32[]{:T(128)}) while((s32[]{:T(128)}, f32[4,3,256]{2,0,1:T(4,128)S(1)}, s32[4,8]{0,1:T(8,128)S(1)}, f32[192,6,256]{2,1,0:T(8,128)S(1)}, ...), condition=%wide.region_8.8_spmd.clone, body=%wide.region_4.7_spmd.clone.sunk | while | flops 6829071 | bytes 262299 | solution.py:110
  360.3 18.1 %while.26 = (s32[]{:T(128)}, f32[4,3,256]{2,0,1:T(4,128)S(1)}, s32[4,8]{0,1:T(8,128)S(1)}, f32[192,6,256]{2,1,0:T(8,128)S(1)}, f32[4,6,256]{2,0,1:T(4,128)S(1)}, /*index=5*/s32[]{:T(128)}, s32[]{:T(128)}) while((s32[]{:T(128)}, f32[4,3,256]{2,0,1:T(4,128)S(1)}, s32[4,8]{0,1:T(8,128)S(1)}, f32[192,6,256]{2,1,0:T(8,128)S(1)}, ...), condition=%wide.region_8.8_spmd.clone, body=%wide.region_4.7_spmd.clone.sunk | while | flops 6829071 | bytes 262299 | solution.py:110
  379.9 18.1 %while.26 = (s32[]{:T(128)}, f32[4,3,256]{2,0,1:T(4,128)S(1)}, s32[4,8]{0,1:T(8,128)S(1)}, f32[192,6,256]{2,1,0:T(8,128)S(1)}, f32[4,6,256]{2,0,1:T(4,128)S(1)}, /*index=5*/s32[]{:T(128)}, s32[]{:T(128)}) while((s32[]{:T(128)}, f32[4,3,256]{2,0,1:T(4,128)S(1)}, s32[4,8]{0,1:T(8,128)S(1)}, f32[192,6,256]{2,1,0:T(8,128)S(1)}, ...), condition=%wide.region_8.8_spmd.clone, body=%wide.region_4.7_spmd.clone.sunk | while | flops 6829071 | bytes 262299 | solution.py:110
  399.4 18.1 %while.26 = (s32[]{:T(128)}, f32[4,3,256]{2,0,1:T(4,128)S(1)}, s32[4,8]{0,1:T(8,128)S(1)}, f32[192,6,256]{2,1,0:T(8,128)S(1)}, f32[4,6,256]{2,0,1:T(4,128)S(1)}, /*index=5*/s32[]{:T(128)}, s32[]{:T(128)}) while((s32[]{:T(128)}, f32[4,3,256]{2,0,1:T(4,128)S(1)}, s32[4,8]{0,1:T(8,128)S(1)}, f32[192,6,256]{2,1,0:T(8,128)S(1)}, ...), condition=%wide.region_8.8_spmd.clone, body=%wide.region_4.7_spmd.clone.sunk | while | flops 6829071 | bytes 262299 | solution.py:110
  418.9 18.1 %while.26 = (s32[]{:T(128)}, f32[4,3,256]{2,0,1:T(4,128)S(1)}, s32[4,8]{0,1:T(8,128)S(1)}, f32[192,6,256]{2,1,0:T(8,128)S(1)}, f32[4,6,256]{2,0,1:T(4,128)S(1)}, /*index=5*/s32[]{:T(128)}, s32[]{:T(128)}) while((s32[]{:T(128)}, f32[4,3,256]{2,0,1:T(4,128)S(1)}, s32[4,8]{0,1:T(8,128)S(1)}, f32[192,6,256]{2,1,0:T(8,128)S(1)}, ...), condition=%wide.region_8.8_spmd.clone, body=%wide.region_4.7_spmd.clone.sunk | while | flops 6829071 | bytes 262299 | solution.py:110
  (1472 shorter events, 282.9 us)
Async XLA Ops:
  0.6 1.9 copy-start
  0.6 27.5 %copy-start.2 = (f32[128,3,256]{2,0,1:T(8,128)S(1)}, f32[128,3,256]{2,0,1:T(8,128)}, u32[]{:S(2)}) copy-start(f32[128,3,256]{2,0,1:T(8,128)} %param.10) | copy-start | bytes 1179652
  0.7 27.8 %copy-start.3 = (f32[128,3,256]{2,0,1:T(8,128)S(1)}, f32[128,3,256]{2,0,1:T(8,128)}, u32[]{:S(2)}) copy-start(f32[128,3,256]{2,0,1:T(8,128)} %param.11) | copy-start | bytes 1179652
  5.3 46.5 %all-to-all-start = ((f32[32,1,4]{2,1,0:T(1,128)}), f32[32,1,4]{2,1,0:T(1,128)S(1)}, u32[]{:S(2)}, u32[]{:S(2)}) async-start(f32[32,1,4]{2,1,0:T(1,128)} %copy.93), calls=%async_computation | async-start | bytes 32768 | tf_op jit(solution)/shard_map/all_to_all | solution.py:72
  12.6 23.9 %collective-permute-start = (s32[16]{0:T(128)S(1)}, s32[16]{0:T(128)S(1)}, u32[]{:S(2)}, u32[]{:S(2)}) collective-permute-start(s32[16]{0:T(128)S(1)} %get-tuple-element.235), channel_id=1, source_target_pairs={{4,0},{8,4},{12,8},{16,12},{20,16},{24,20},{28,24},{5,1},{9,5},{13... | collective-permute-start | bytes 200 | tf_op jit(solution)/shard_map/ppermute | solution.py:16
  14.8 16.2 %collective-permute-start.4 = (s32[16]{0:T(128)S(1)}, s32[16]{0:T(128)S(1)}, u32[]{:S(2)}, u32[]{:S(2)}) collective-permute-start(s32[16]{0:T(128)S(1)} %get-tuple-element.234), channel_id=1, source_target_pairs={{4,0},{8,4},{12,8},{16,12},{20,16},{24,20},{28,24},{5,1},{9,5},{13... | collective-permute-start | bytes 200 | tf_op jit(solution)/shard_map/ppermute | solution.py:16
  17.9 22.6 %collective-permute-start.6 = (s32[16]{0:T(128)S(1)}, s32[16]{0:T(128)S(1)}, u32[]{:S(2)}, u32[]{:S(2)}) collective-permute-start(s32[16]{0:T(128)S(1)} %get-tuple-element.233), channel_id=1, source_target_pairs={{4,0},{8,4},{12,8},{16,12},{20,16},{24,20},{28,24},{5,1},{9,5},{13... | collective-permute-start | bytes 200 | tf_op jit(solution)/shard_map/ppermute | solution.py:16
  19.9 14.4 %collective-permute-start.10 = (s32[16]{0:T(128)S(1)}, s32[16]{0:T(128)S(1)}, u32[]{:S(2)}, u32[]{:S(2)}) collective-permute-start(s32[16]{0:T(128)S(1)} %get-tuple-element.232), channel_id=1, source_target_pairs={{1,0},{2,1},{3,2},{5,4},{6,5},{7,6},{9,8},{10,9},{11,10},{13,12},{... | collective-permute-start | bytes 200 | tf_op jit(solution)/shard_map/ppermute | solution.py:16
  22.9 19.5 %collective-permute-start.14 = (s32[16]{0:T(128)S(1)}, s32[16]{0:T(128)S(1)}, u32[]{:S(2)}, u32[]{:S(2)}) collective-permute-start(s32[16]{0:T(128)S(1)} %get-tuple-element.230), channel_id=1, source_target_pairs={{0,4},{4,8},{8,12},{12,16},{16,20},{20,24},{24,28},{1,5},{5,9},{9,... | collective-permute-start | bytes 200 | tf_op jit(solution)/shard_map/ppermute | solution.py:16
  31.0 15.1 %collective-permute-start.12 = (s32[16]{0:T(128)S(1)}, s32[16]{0:T(128)S(1)}, u32[]{:S(2)}, u32[]{:S(2)}) collective-permute-start(s32[16]{0:T(128)S(1)} %get-tuple-element.231), channel_id=1, source_target_pairs={{0,1},{1,2},{2,3},{4,5},{5,6},{6,7},{8,9},{9,10},{10,11},{12,13},{... | collective-permute-start | bytes 200 | tf_op jit(solution)/shard_map/ppermute | solution.py:16
  34.3 13.8 %collective-permute-start.20 = (s32[16]{0:T(128)S(1)}, s32[16]{0:T(128)S(1)}, u32[]{:S(2)}, u32[]{:S(2)}) collective-permute-start(s32[16]{0:T(128)S(1)} %get-tuple-element.229), channel_id=1, source_target_pairs={{0,4},{4,8},{8,12},{12,16},{16,20},{20,24},{24,28},{1,5},{5,9},{9,... | collective-permute-start | bytes 200 | tf_op jit(solution)/shard_map/ppermute | solution.py:16
  36.5 15.2 %collective-permute-start.18 = (s32[16]{0:T(128)S(1)}, s32[16]{0:T(128)S(1)}, u32[]{:S(2)}, u32[]{:S(2)}) collective-permute-start(s32[16]{0:T(128)S(1)} %get-tuple-element.236), channel_id=1, source_target_pairs={{0,4},{4,8},{8,12},{12,16},{16,20},{20,24},{24,28},{1,5},{5,9},{9,... | collective-permute-start | bytes 200 | tf_op jit(solution)/shard_map/ppermute | solution.py:16
  40.5 11.2 %collective-permute-start.1 = (s32[16]{0:T(128)S(1)}, s32[16]{0:T(128)S(1)}, u32[]{:S(2)}, u32[]{:S(2)}) collective-permute-start(s32[16]{0:T(128)S(1)} %collective-permute-done), channel_id=1, source_target_pairs={{1,0},{2,1},{3,2},{5,4},{6,5},{7,6},{9,8},{10,9},{11,10},{13,12},{... | collective-permute-start | bytes 200 | tf_op jit(solution)/shard_map/ppermute | solution.py:16
  42.5 12.1 %collective-permute-start.7 = (s32[16]{0:T(128)S(1)}, s32[16]{0:T(128)S(1)}, u32[]{:S(2)}, u32[]{:S(2)}) collective-permute-start(s32[16]{0:T(128)S(1)} %collective-permute-done.6), channel_id=1, source_target_pairs={{0,1},{1,2},{2,3},{4,5},{5,6},{6,7},{8,9},{9,10},{10,11},{12,13},{... | collective-permute-start | bytes 200 | tf_op jit(solution)/shard_map/ppermute | solution.py:16
  46.1 8.5 %collective-permute-start.15 = (s32[16]{0:T(128)S(1)}, s32[16]{0:T(128)S(1)}, u32[]{:S(2)}, u32[]{:S(2)}) collective-permute-start(s32[16]{0:T(128)S(1)} %collective-permute-done.14), channel_id=1, source_target_pairs={{1,0},{2,1},{3,2},{5,4},{6,5},{7,6},{9,8},{10,9},{11,10},{13,12},{... | collective-permute-start | bytes 200 | tf_op jit(solution)/shard_map/ppermute | solution.py:16
  48.1 6.6 %collective-permute-start.21 = (s32[16]{0:T(128)S(1)}, s32[16]{0:T(128)S(1)}, u32[]{:S(2)}, u32[]{:S(2)}) collective-permute-start(s32[16]{0:T(128)S(1)} %collective-permute-done.20), channel_id=1, source_target_pairs={{0,1},{1,2},{2,3},{4,5},{5,6},{6,7},{8,9},{9,10},{10,11},{12,13},{... | collective-permute-start | bytes 200 | tf_op jit(solution)/shard_map/ppermute | solution.py:16
  51.8 21.3 %all-to-all-start.1 = ((f32[32,4,6,256]{3,1,2,0:T(4,128)}), f32[32,4,6,256]{3,1,2,0:T(4,128)S(1)}, u32[]{:S(2)}, u32[]{:S(2)}) async-start(f32[32,4,6,256]{3,1,2,0:T(4,128)} %copy_multiply_fusion), calls=%async_computation.1 | async-start | bytes 1572864 | tf_op jit(solution)/shard_map/all_to_all | solution.py:71
  75.3 6.6 %collective-permute-start.2 = (f32[16,6,256]{2,0,1:T(8,128)S(1)}, f32[16,6,256]{2,0,1:T(8,128)}, u32[]{:S(2)}, u32[]{:S(2)}) collective-permute-start(f32[16,6,256]{2,0,1:T(8,128)S(1)} %copy.101), channel_id=1, source_target_pairs={{0,4},{4,8},{8,12},{12,16},{16,20},{20,24},{24,28},{1,5},{5,9},{9,... | collective-permute-start | bytes 294920 | tf_op jit(solution)/shard_map/ppermute | solution.py:16
  81.8 18.4 %collective-permute-start.3 = (f32[16,6,256]{2,0,1:T(8,128)}, f32[16,6,256]{2,0,1:T(8,128)}, u32[]{:S(2)}, u32[]{:S(2)}) collective-permute-start(f32[16,6,256]{2,0,1:T(8,128)} %collective-permute-done.2), channel_id=1, source_target_pairs={{0,1},{1,2},{2,3},{4,5},{5,6},{6,7},{8,9},{9,10},{10,11},{12,13},{... | collective-permute-start | bytes 294920 | tf_op jit(solution)/shard_map/ppermute | solution.py:16
  86.3 18.3 %collective-permute-start.5 = (f32[16,6,256]{2,0,1:T(8,128)S(1)}, f32[16,6,256]{2,0,1:T(8,128)S(1)}, u32[]{:S(2)}, u32[]{:S(2)}) collective-permute-start(f32[16,6,256]{2,0,1:T(8,128)S(1)} %copy.103), channel_id=1, source_target_pairs={{0,4},{4,8},{8,12},{12,16},{16,20},{20,24},{24,28},{1,5},{5,9},{9,... | collective-permute-start | bytes 294920 | tf_op jit(solution)/shard_map/ppermute | solution.py:16
  90.9 16.7 %collective-permute-start.8 = (f32[16,6,256]{2,0,1:T(8,128)S(1)}, f32[16,6,256]{2,0,1:T(8,128)}, u32[]{:S(2)}, u32[]{:S(2)}) collective-permute-start(f32[16,6,256]{2,0,1:T(8,128)S(1)} %copy.105), channel_id=1, source_target_pairs={{0,4},{4,8},{8,12},{12,16},{16,20},{20,24},{24,28},{1,5},{5,9},{9,... | collective-permute-start | bytes 294920 | tf_op jit(solution)/shard_map/ppermute | solution.py:16
  93.4 26.7 %collective-permute-start.11 = (f32[16,6,256]{2,0,1:T(8,128)S(1)}, f32[16,6,256]{2,0,1:T(8,128)S(1)}, u32[]{:S(2)}, u32[]{:S(2)}) collective-permute-start(f32[16,6,256]{2,0,1:T(8,128)S(1)} %copy.107), channel_id=1, source_target_pairs={{0,1},{1,2},{2,3},{4,5},{5,6},{6,7},{8,9},{9,10},{10,11},{12,13},{... | collective-permute-start | bytes 294920 | tf_op jit(solution)/shard_map/ppermute | solution.py:16
  96.2 23.9 %collective-permute-start.13 = (f32[16,6,256]{2,0,1:T(8,128)S(1)}, f32[16,6,256]{2,0,1:T(8,128)S(1)}, u32[]{:S(2)}, u32[]{:S(2)}) collective-permute-start(f32[16,6,256]{2,0,1:T(8,128)S(1)} %copy.109), channel_id=1, source_target_pairs={{1,0},{2,1},{3,2},{5,4},{6,5},{7,6},{9,8},{10,9},{11,10},{13,12},{... | collective-permute-start | bytes 294920 | tf_op jit(solution)/shard_map/ppermute | solution.py:16
  100.2 9.3 %collective-permute-start.16 = (f32[16,6,256]{2,0,1:T(8,128)S(1)}, f32[16,6,256]{2,0,1:T(8,128)S(1)}, u32[]{:S(2)}, u32[]{:S(2)}) collective-permute-start(f32[16,6,256]{2,0,1:T(8,128)S(1)} %copy.111), channel_id=1, source_target_pairs={{4,0},{8,4},{12,8},{16,12},{20,16},{24,20},{28,24},{5,1},{9,5},{13... | collective-permute-start | bytes 294920 | tf_op jit(solution)/shard_map/ppermute | solution.py:16
  104.6 9.0 %collective-permute-start.22 = (f32[16,6,256]{2,0,1:T(8,128)S(1)}, f32[16,6,256]{2,0,1:T(8,128)S(1)}, u32[]{:S(2)}, u32[]{:S(2)}) collective-permute-start(f32[16,6,256]{2,0,1:T(8,128)S(1)} %copy.115), channel_id=1, source_target_pairs={{4,0},{8,4},{12,8},{16,12},{20,16},{24,20},{28,24},{5,1},{9,5},{13... | collective-permute-start | bytes 294920 | tf_op jit(solution)/shard_map/ppermute | solution.py:16
  107.6 10.5 %collective-permute-start.9 = (f32[16,6,256]{2,0,1:T(8,128)}, f32[16,6,256]{2,0,1:T(8,128)S(1)}, u32[]{:S(2)}, u32[]{:S(2)}) collective-permute-start(f32[16,6,256]{2,0,1:T(8,128)} %collective-permute-done.8), channel_id=1, source_target_pairs={{1,0},{2,1},{3,2},{5,4},{6,5},{7,6},{9,8},{10,9},{11,10},{13,12},{... | collective-permute-start | bytes 294920 | tf_op jit(solution)/shard_map/ppermute | solution.py:16
  109.6 10.6 %collective-permute-start.19 = (f32[16,6,256]{2,0,1:T(8,128)S(1)}, f32[16,6,256]{2,0,1:T(8,128)S(1)}, u32[]{:S(2)}, u32[]{:S(2)}) collective-permute-start(f32[16,6,256]{2,0,1:T(8,128)S(1)} %copy.113), channel_id=1, source_target_pairs={{4,0},{8,4},{12,8},{16,12},{20,16},{24,20},{28,24},{5,1},{9,5},{13... | collective-permute-start | bytes 294920 | tf_op jit(solution)/shard_map/ppermute | solution.py:16
  113.6 6.5 %collective-permute-start.17 = (f32[16,6,256]{2,0,1:T(8,128)S(1)}, f32[16,6,256]{2,0,1:T(8,128)S(1)}, u32[]{:S(2)}, u32[]{:S(2)}) collective-permute-start(f32[16,6,256]{2,0,1:T(8,128)S(1)} %collective-permute-done.16), channel_id=1, source_target_pairs={{0,1},{1,2},{2,3},{4,5},{5,6},{6,7},{8,9},{9,10},{10,11},{12,13},{... | collective-permute-start | bytes 294920 | tf_op jit(solution)/shard_map/ppermute | solution.py:16
  118.1 5.9 %collective-permute-start.23 = (f32[16,6,256]{2,0,1:T(8,128)S(1)}, f32[16,6,256]{2,0,1:T(8,128)S(1)}, u32[]{:S(2)}, u32[]{:S(2)}) collective-permute-start(f32[16,6,256]{2,0,1:T(8,128)S(1)} %collective-permute-done.22), channel_id=1, source_target_pairs={{1,0},{2,1},{3,2},{5,4},{6,5},{7,6},{9,8},{10,9},{11,10},{13,12},{... | collective-permute-start | bytes 294920 | tf_op jit(solution)/shard_map/ppermute | solution.py:16
  124.1 0.7 copy-start.4
  437.0 0.8 copy-start.1
where the time goes:
time: 439 us; the launch traced here: 438 us
  other arithmetic  209 us (48%)
  local copies, waits for them, and re-layouts  101 us (23%)
  starting transfers between devices  81.2 us (18%)
  loops' own time  22.2 us (5%)
  waiting for transfers between devices  22.1 us (5%)
    reduce_sum x128, other arithmetic, induced(): jnp.sum((alpha_y * delta_z - alpha_z * delta_y) * inverse_cube, axis=2)  199 us
    ppermute x24, starting transfers between devices, shifted(): return lax.ppermute(shard, axis, pairs)  72.1 us
    gather x128, local copies, waits for them, and re-layouts, add_neighbour(): sources = combined[column]  70.5 us
    all_to_all x1, waiting for transfers between devices, local(): lax.all_to_all(outgoing, ('bx', 'by'), split_axis=0, concat_axis=0, tiled...  15.8 us
    another operation x1, loops' own time, local(): lax.map(one_block, jnp.arange(turns, dtype=jnp.int32)).reshape(own, 3, leaf)  11.2 us
    another operation x16, loops' own time, one_block(): summed = lax.fori_loop(0, near_count, add_neighbour, start_total)  11 us
    dynamic_slice x16, local copies, waits for them, and re-layouts, local(): lax.map(one_block, jnp.arange(turns, dtype=jnp.int32)).reshape(own, 3, leaf)  9.38 us
  transfers between devices with their start and end apart: 26, of which 3 were waited for; matrix products, arithmetic and copies ran while one was open for 3% of the time, Pallas kernels for 0%

commit v1 on v0

v1 whole, which is shorter than its diff:
```python
import functools
import math

import jax
import jax.numpy as jnp
from jax import lax
from jax.experimental import pallas as pl
from jax.experimental.pallas import tpu as pltpu
from jax.sharding import PartitionSpec as P

CORE_SQUARED = 0.01
OFFSET_ROWS = (-1, -1, -1, 0, 0, 1, 1, 1)
OFFSET_COLS = (-1, 0, 1, -1, 1, -1, 0, 1)

def shifted(values, off_a, off_b, rows_bx, rows_by):
    pairs = []
    for a in range(rows_bx):
        for b in range(rows_by):
            if 0 <= a + off_a < rows_bx and 0 <= b + off_b < rows_by:
                pairs.append((a * rows_by + b, (a + off_a) * rows_by + b + off_b))
    return lax.ppermute(values, ("bx", "by"), pairs)


def split3(value):
    first = value.astype(jnp.bfloat16).astype(jnp.float32)
    rest = value - first
    second = rest.astype(jnp.bfloat16).astype(jnp.float32)
    return first, second, rest - second


def near_field(own, near, count, combined, velocity, features, moments):
    leaf = velocity.shape[2]
    near_count = near.shape[1]

    def add_corner(index, total):
        return total + combined[index, 0:3, :]

    middle = lax.fori_loop(0, own, add_corner, jnp.zeros((3, leaf), jnp.float32))[:, 0:1] / own
    ones = jnp.ones((1, leaf), jnp.float32)
    padding = jnp.zeros((8, leaf), jnp.float32)

    def prepare(index, carry):
        x = combined[index, 0:3, :] - middle
        alpha = combined[index, 3:6, :]
        a, b, c = split3(x)
        n1, n2, n3 = split3(jnp.sum(x * x, axis=0, keepdims=True))
        rows = jnp.concatenate([a, a, a, b, b, c, n1, n2, n3, ones, ones, ones, padding], axis=0)
        features[index] = rows.T.astype(jnp.bfloat16)
        moment_x = alpha[1:2] * x[2:3] - alpha[2:3] * x[1:2]
        moment_y = alpha[2:3] * x[0:1] - alpha[0:1] * x[2:3]
        moment_z = alpha[0:1] * x[1:2] - alpha[1:2] * x[0:1]
        rows = jnp.concatenate([alpha, moment_x, moment_y, moment_z, padding[0:2]], axis=0)
        high = rows.astype(jnp.bfloat16).astype(jnp.float32)
        moments[index] = jnp.concatenate([high, rows - high], axis=0).astype(jnp.bfloat16)
        return carry

    lax.fori_loop(0, combined.shape[0], prepare, 0)

    def target(index, carry):
        x = combined[index, 0:3, :] - middle
        a, b, c = split3(x)
        n1, n2, n3 = split3(jnp.sum(x * x, axis=0, keepdims=True) + CORE_SQUARED)
        rows = jnp.concatenate(
            [-2.0 * a, -2.0 * b, -2.0 * c, -2.0 * a, -2.0 * b, -2.0 * a, ones, ones, ones, n1, n2, n3, padding],
            axis=0,
        ).astype(jnp.bfloat16)
        total = jnp.zeros((16, leaf), jnp.float32)
        for entry in range(near_count):
            source = near[index, entry]
            squared = jnp.dot(features[source], rows, preferred_element_type=jnp.float32)
            inverse = lax.rsqrt(squared)
            weight = inverse * inverse * inverse
            high = weight.astype(jnp.bfloat16)
            low = (weight - high.astype(jnp.float32)).astype(jnp.bfloat16)
            left = moments[source]
            total = (
                total
                + jnp.dot(left, high, preferred_element_type=jnp.float32)
                + jnp.dot(left, low, preferred_element_type=jnp.float32)
            )
        sums = total[0:8] + total[8:16]
        speed = jnp.concatenate(
            [
                sums[1:2] * x[2:3] - sums[2:3] * x[1:2],
                sums[2:3] * x[0:1] - sums[0:1] * x[2:3],
                sums[0:1] * x[1:2] - sums[1:2] * x[0:1],
            ],
            axis=0,
        ) - sums[3:6]
        live = lax.broadcasted_iota(jnp.int32, (3, leaf), 1) < count[index]
        velocity[index] = jnp.where(live, speed * (0.25 / math.pi), 0.0)
        return carry

    lax.fori_loop(0, own, target, 0)


def local(positions, strengths, blob_count, split_counts, ghost_ids, near_list):
    rows_bx = lax.axis_size("bx")
    rows_by = lax.axis_size("by")
    devices = rows_bx * rows_by
    slots = positions.shape[0]
    pair_most = slots // devices
    leaf = positions.shape[2]
    own = near_list.shape[0]
    requests = [
        shifted(ghost_ids[0, direction], OFFSET_ROWS[direction], OFFSET_COLS[direction], rows_bx, rows_by)
        for direction in range(8)
    ]
    counts_row = split_counts[0]
    starts = jnp.cumsum(counts_row) - counts_row
    within = jnp.arange(pair_most, dtype=jnp.int32)
    pick = jnp.minimum(starts[:, None] + within[None, :], slots - 1).reshape(-1)
    valid = (within[None, :] < counts_row[:, None]).reshape(-1)
    stacked = jnp.concatenate([positions, strengths], axis=1)[pick]
    sent_count = jnp.where(valid, blob_count[pick], 0)
    sent_live = (jnp.arange(leaf, dtype=jnp.int32)[None, :] < sent_count[:, None]).astype(
        jnp.float32
    )
    outgoing = (stacked * sent_live[:, None, :]).reshape(devices, pair_most, 6, leaf)
    out_count = sent_count.astype(jnp.float32).reshape(devices, pair_most)
    arrived, arrived_count = (
        lax.all_to_all(outgoing, ("bx", "by"), split_axis=0, concat_axis=0, tiled=True),
        lax.all_to_all(out_count, ("bx", "by"), split_axis=0, concat_axis=0, tiled=True),
    )
    arrived_valid = arrived_count > 0.0
    per_source = jnp.sum(arrived_valid.astype(jnp.int32), axis=1)
    prefix = jnp.cumsum(per_source) - per_source
    placed = jnp.where(arrived_valid, prefix[:, None] + within[None, :], own).reshape(-1)
    selector = (jnp.arange(own, dtype=jnp.int32)[:, None] == placed[None, :]).astype(jnp.float32)
    owned_blobs = jnp.dot(
        selector, arrived.reshape(devices * pair_most, 6 * leaf), precision=lax.Precision.HIGHEST
    ).reshape(own, 6, leaf)
    own_count = jnp.dot(selector, arrived_count.reshape(-1), precision=lax.Precision.HIGHEST)
    ghost_blocks = []
    for direction in range(8):
        served = owned_blobs[requests[direction]]
        ghost_blocks.append(
            shifted(served, -OFFSET_ROWS[direction], -OFFSET_COLS[direction], rows_bx, rows_by)
        )
    combined = jnp.concatenate([owned_blobs] + ghost_blocks, axis=0)
    smem = pl.BlockSpec(memory_space=pltpu.SMEM)
    vmem = pl.BlockSpec(memory_space=pltpu.VMEM)
    velocity = pl.pallas_call(
        functools.partial(near_field, own),
        out_shape=jax.ShapeDtypeStruct((own, 3, leaf), jnp.float32),
        in_specs=[smem, smem, vmem],
        out_specs=vmem,
        scratch_shapes=[
            pltpu.VMEM((combined.shape[0], leaf, 32), jnp.bfloat16),
            pltpu.VMEM((combined.shape[0], 16, leaf), jnp.bfloat16),
        ],
        compiler_params=pltpu.CompilerParams(vmem_limit_bytes=48 * 1024 * 1024),
        name="near_field",
    )(near_list, own_count.astype(jnp.int32), combined)
    return (owned_blobs, velocity)


def solution(mesh):
    placed = (
        P(("bx", "by"), None, None),
        P(("bx", "by"), None, None),
        P(("bx", "by")),
        P(("bx", "by"), None),
        P(("bx", "by"), None, None),
        P(("bx", "by"), None),
    )
    return jax.shard_map(
        local,
        mesh=mesh,
        in_specs=placed,
        out_specs=(P(("bx", "by"), None, None), P(("bx", "by"), None, None)),
        check_vma=False,
    )
```

time: 439 us -> 204 us (0.46)
  other arithmetic: 209 us -> 5.55 us
  Pallas kernels: 0 us -> 97.1 us
  local copies, waits for them, and re-layouts: 101 us -> 17.5 us
  loops' own time: 22.2 us -> 0 us
  starting transfers between devices: 81.2 us -> 59.3 us
    reduce_sum x128 -> x0, other arithmetic: 199 us -> none  [induced(): jnp.sum((alpha_y * delta_z - alpha_z * delta_y) * inverse_cube, axis=2)]
    pallas_call x0 -> x1, Pallas kernels: none -> 97.1 us  [local(): pl.pallas_call(functools.partial(near_field, own), out_shape=jax.ShapeDty...]
    gather x144 -> x8, local copies, waits for them, and re-layouts: 75.2 us -> 6.51 us  [local(): served = owned_blobs[requests[direction]]]
    ppermute x24 -> x16, starting transfers between devices: 72.1 us -> 49.3 us  [shifted(): return lax.ppermute(values, ('bx', 'by'), pairs)]
    another operation x17 -> x0, loops' own time: 22.2 us -> none  [the longest x1 11.2 us: local(): lax.map(one_block, jnp.arange(turns, dtype=jnp.int32)).reshape(own, 3, leaf)]
    dynamic_slice x64 -> x0, local copies, waits for them, and re-layouts: 11 us -> none  [the longest x16 9.38 us: local(): lax.map(one_block, jnp.arange(turns, dtype=jnp.int32)).reshape(own, 3, leaf)]
  transfers between devices with their start and end apart: 26 -> 18, of which waited for: 3 -> 3; matrix products, arithmetic and copies ran while one was open for 3% -> 8% of each run, Pallas kernels for 0% -> 0%
where the time goes in v1:
time: 204 us; the launch traced here: 203 us
  Pallas kernels  97.1 us (48%)
  starting transfers between devices  59.3 us (29%)
  waiting for transfers between devices  21.9 us (11%)
  local copies, waits for them, and re-layouts  17.5 us (9%)
  other arithmetic  5.55 us (3%)
    pallas_call x1, Pallas kernels, local(): pl.pallas_call(functools.partial(near_field, own), out_shape=jax.ShapeDty...  97.1 us
    ppermute x16, starting transfers between devices, shifted(): return lax.ppermute(values, ('bx', 'by'), pairs)  49.3 us
    all_to_all x1, waiting for transfers between devices, local(): lax.all_to_all(outgoing, ('bx', 'by'), split_axis=0, concat_axis=0, tiled...  15.8 us
    gather x8, local copies, waits for them, and re-layouts, local(): served = owned_blobs[requests[direction]]  6.51 us
    all_to_all x1, starting transfers between devices, local(): lax.all_to_all(out_count, ('bx', 'by'), split_axis=0, concat_axis=0, tile...  6.33 us
    ppermute x16, waiting for transfers between devices, shifted(): return lax.ppermute(values, ('bx', 'by'), pairs)  6.07 us
    unnamed x20, local copies, waits for them, and re-layouts  4.51 us
  transfers between devices with their start and end apart: 18, of which 3 were waited for; matrix products, arithmetic and copies ran while one was open for 8% of the time, Pallas kernels for 0%

profile of v1, /device:TPU:11, one launch (start us, length us, event | category | flops | bytes accessed | tf_op | source)
XLA Modules:
  0.0 203.3 jit_solution(13491674213017513616)
XLA Ops:
  0.7 0.8 copy.49
  1.5 0.1 reduce.1
  1.6 0.7 bitcast_subtract_fusion
  2.4 0.1 min.19
  2.5 1.2 gather_fusion
  3.7 0.1 gather.37
  3.9 0.7 select_convert_fusion
  4.6 0.7 copy.51
  5.3 6.3 %all-to-all-start = ((f32[32,1,4]{2,1,0:T(1,128)}), f32[32,1,4]{2,1,0:T(1,128)S(1)}, u32[]{:S(2)}, u32[]{:S(2)}) async-start(f32[32,1,4]{2,1,0:T(1,128)} %copy.51), calls=%async_computation | async-start | bytes 32768 | tf_op jit(solution)/shard_map/all_to_all | solution.py:123
  11.6 1.0 slice_bitcast_fusion
  12.6 2.2 %collective-permute-start.2 = (s32[16]{0:T(128)S(1)}, s32[16]{0:T(128)S(1)}, u32[]{:S(2)}, u32[]{:S(2)}) collective-permute-start(s32[16]{0:T(128)S(1)} %get-tuple-element.17), channel_id=1, source_target_pairs={{4,0},{5,1},{6,2},{7,3},{8,4},{9,5},{10,6},{11,7},{12,8},{13,9},{1... | collective-permute-start | bytes 200 | tf_op jit(solution)/shard_map/ppermute | solution.py:21
  14.8 3.6 %collective-permute-start = (s32[16]{0:T(128)S(1)}, s32[16]{0:T(128)S(1)}, u32[]{:S(2)}, u32[]{:S(2)}) collective-permute-start(s32[16]{0:T(128)S(1)} %get-tuple-element.18), channel_id=1, source_target_pairs={{5,0},{6,1},{7,2},{9,4},{10,5},{11,6},{13,8},{14,9},{15,10},{17,12... | collective-permute-start | bytes 200 | tf_op jit(solution)/shard_map/ppermute | solution.py:21
  18.4 1.9 collective-permute-start.6
  20.3 3.3 %collective-permute-start.4 = (s32[16]{0:T(128)S(1)}, s32[16]{0:T(128)S(1)}, u32[]{:S(2)}, u32[]{:S(2)}) collective-permute-start(s32[16]{0:T(128)S(1)} %get-tuple-element.16), channel_id=1, source_target_pairs={{4,1},{5,2},{6,3},{8,5},{9,6},{10,7},{12,9},{13,10},{14,11},{16,13... | collective-permute-start | bytes 200 | tf_op jit(solution)/shard_map/ppermute | solution.py:21
  23.7 3.1 %collective-permute-start.10 = (s32[16]{0:T(128)S(1)}, s32[16]{0:T(128)S(1)}, u32[]{:S(2)}, u32[]{:S(2)}) collective-permute-start(s32[16]{0:T(128)S(1)} %get-tuple-element.13), channel_id=1, source_target_pairs={{1,4},{2,5},{3,6},{5,8},{6,9},{7,10},{9,12},{10,13},{11,14},{13,16... | collective-permute-start | bytes 200 | tf_op jit(solution)/shard_map/ppermute | solution.py:21
  26.8 0.1 gather.40
  26.9 0.7 fusion.8
  27.6 0.1 fusion.1
  27.8 1.3 copy.53
  29.0 0.3 copy.54
  29.3 0.2 pad_maximum_fusion
  29.5 0.8 gather_fusion.1
  30.3 1.3 copy_multiply_fusion
  31.7 4.5 %collective-permute-start.8 = (s32[16]{0:T(128)S(1)}, s32[16]{0:T(128)S(1)}, u32[]{:S(2)}, u32[]{:S(2)}) collective-permute-start(s32[16]{0:T(128)S(1)} %get-tuple-element.14), channel_id=1, source_target_pairs={{0,1},{1,2},{2,3},{4,5},{5,6},{6,7},{8,9},{9,10},{10,11},{12,13},{... | collective-permute-start | bytes 200 | tf_op jit(solution)/shard_map/ppermute | solution.py:21
  36.2 1.9 collective-permute-start.14
  38.2 4.0 %collective-permute-start.12 = (s32[16]{0:T(128)S(1)}, s32[16]{0:T(128)S(1)}, u32[]{:S(2)}, u32[]{:S(2)}) collective-permute-start(s32[16]{0:T(128)S(1)} %get-tuple-element.19), channel_id=1, source_target_pairs={{0,4},{1,5},{2,6},{3,7},{4,8},{5,9},{6,10},{7,11},{8,12},{9,13},{1... | collective-permute-start | bytes 200 | tf_op jit(solution)/shard_map/ppermute | solution.py:21
  42.3 3.6 %all-to-all-start.1 = ((f32[32,4,6,256]{3,1,2,0:T(4,128)}), f32[32,4,6,256]{3,1,2,0:T(4,128)S(1)}, u32[]{:S(2)}, u32[]{:S(2)}) async-start(f32[32,4,6,256]{3,1,2,0:T(4,128)} %copy_multiply_fusion), calls=%async_computation.1 | async-start | bytes 1572864 | tf_op jit(solution)/shard_map/all_to_all | solution.py:122
  46.0 0.7 fusion.5
  46.7 0.1 copy.52
  46.8 0.1 reduce.3
  47.0 0.1 add.78
  47.1 0.5 broadcast.169
  47.6 0.7 reduce.8
  48.3 0.1 all_to_all.10
  48.4 0.1 reshape.311
  48.6 15.8 %all-to-all-done.1 = f32[32,4,6,256]{3,1,2,0:T(4,128)S(1)} async-done(((f32[32,4,6,256]{3,1,2,0:T(4,128)}), f32[32,4,6,256]{3,1,2,0:T(4,128)S(1)}, u32[]{:S(2)}, u32[]{:S(2)}) %all-to-all-start.1) | async-done | bytes 786464 | tf_op jit(solution)/shard_map/all_to_all | solution.py:122
  64.4 0.2 copy.56
  64.6 0.3 copy.69
  64.8 0.3 copy.57
  65.1 0.6 fusion.3
  65.7 0.2 fusion.10
  66.0 1.2 gather_fusion.2
  67.2 4.6 %collective-permute-start.1 = (f32[16,6,256]{2,1,0:T(8,128)}, f32[16,6,256]{2,1,0:T(8,128)}, u32[]{:S(2)}, u32[]{:S(2)}) collective-permute-start(f32[16,6,256]{2,1,0:T(8,128)} %gather_fusion.2), channel_id=1, source_target_pairs={{0,5},{1,6},{2,7},{4,9},{5,10},{6,11},{8,13},{9,14},{10,15},{12,17... | collective-permute-start | bytes 294920 | tf_op jit(solution)/shard_map/ppermute | solution.py:21
  71.8 0.1 fusion.count
  71.9 1.3 gather_fusion.3
  73.1 1.9 collective-permute-start.3
  75.1 1.2 gather_fusion.4
  76.3 3.5 %collective-permute-start.5 = (f32[16,6,256]{2,1,0:T(8,128)}, f32[16,6,256]{2,1,0:T(8,128)S(1)}, u32[]{:S(2)}, u32[]{:S(2)}) collective-permute-start(f32[16,6,256]{2,1,0:T(8,128)} %gather_fusion.4), channel_id=1, source_target_pairs={{1,4},{2,5},{3,6},{5,8},{6,9},{7,10},{9,12},{10,13},{11,14},{13,16... | collective-permute-start | bytes 294920 | tf_op jit(solution)/shard_map/ppermute | solution.py:21
  79.8 0.6 gather_fusion.5
  80.4 3.8 %collective-permute-start.7 = (f32[16,6,256]{2,1,0:T(8,128)S(1)}, f32[16,6,256]{2,1,0:T(8,128)S(1)}, u32[]{:S(2)}, u32[]{:S(2)}) collective-permute-start(f32[16,6,256]{2,1,0:T(8,128)S(1)} %gather_fusion.5), channel_id=1, source_target_pairs={{0,1},{1,2},{2,3},{4,5},{5,6},{6,7},{8,9},{9,10},{10,11},{12,13},{... | collective-permute-start | bytes 294920 | tf_op jit(solution)/shard_map/ppermute | solution.py:21
  84.2 0.6 gather_fusion.6
  84.7 1.9 collective-permute-start.9
  86.7 0.6 gather_fusion.7
  87.2 0.6 gather_fusion.8
  87.8 0.6 gather_fusion.9
  88.4 2.8 %collective-permute-start.11 = (f32[16,6,256]{2,1,0:T(8,128)S(1)}, f32[16,6,256]{2,1,0:T(8,128)S(1)}, u32[]{:S(2)}, u32[]{:S(2)}) collective-permute-start(f32[16,6,256]{2,1,0:T(8,128)S(1)} %gather_fusion.7), channel_id=1, source_target_pairs={{4,1},{5,2},{6,3},{8,5},{9,6},{10,7},{12,9},{13,10},{14,11},{16,13... | collective-permute-start | bytes 294920 | tf_op jit(solution)/shard_map/ppermute | solution.py:21
  91.2 0.9 constant_dynamic-update-slice_fusion.7
  92.1 4.3 %collective-permute-start.13 = (f32[16,6,256]{2,1,0:T(8,128)S(1)}, f32[16,6,256]{2,1,0:T(8,128)S(1)}, u32[]{:S(2)}, u32[]{:S(2)}) collective-permute-start(f32[16,6,256]{2,1,0:T(8,128)S(1)} %gather_fusion.8), channel_id=1, source_target_pairs={{4,0},{5,1},{6,2},{7,3},{8,4},{9,5},{10,6},{11,7},{12,8},{13,9},{1... | collective-permute-start | bytes 294920 | tf_op jit(solution)/shard_map/ppermute | solution.py:21
  96.4 0.9 constant_dynamic-update-slice_fusion.6
  97.3 1.9 collective-permute-start.15
  99.4 0.5 collective-permute-done.13
  99.9 5.5 %collective-permute-done.15 = f32[16,6,256]{2,1,0:T(8,128)S(1)} collective-permute-done((f32[16,6,256]{2,1,0:T(8,128)S(1)}, f32[16,6,256]{2,1,0:T(8,128)S(1)}, u32[]{:S(2)}, u32[]{:S(2)}) %collective-permute-start.15) | collective-permute-done | bytes 98336 | tf_op jit(solution)/shard_map/ppermute | solution.py:21
  105.4 97.1 %near_field.1 = f32[64,3,256]{2,1,0:T(4,128)S(1)} custom-call(s32[64,8]{1,0:T(8,128)S(1)} %copy.67.near, s32[64]{0:T(128)S(1)} %fusion.count, f32[192,6,256]{2,1,0:T(8,128)S(1)} %constant_dynamic-update-slice_fusion.combined), custom_call_target="tpu_custom_call" | custom-call | tf_op jit(solution)/shard_map/near_field/pallas_call | solution.py:143
  202.6 0.7 copy.68
  (51 shorter events, 0.6 us)
Async XLA Ops:
  0.6 1.9 copy-start
  0.6 28.4 %copy-start.2 = (f32[128,3,256]{2,0,1:T(8,128)S(1)}, f32[128,3,256]{2,0,1:T(8,128)}, u32[]{:S(2)}) copy-start(f32[128,3,256]{2,0,1:T(8,128)} %param.7) | copy-start | bytes 1179652
  5.3 37.0 %all-to-all-start = ((f32[32,1,4]{2,1,0:T(1,128)}), f32[32,1,4]{2,1,0:T(1,128)S(1)}, u32[]{:S(2)}, u32[]{:S(2)}) async-start(f32[32,1,4]{2,1,0:T(1,128)} %copy.51), calls=%async_computation | async-start | bytes 32768 | tf_op jit(solution)/shard_map/all_to_all | solution.py:123
  12.6 19.1 %collective-permute-start.2 = (s32[16]{0:T(128)S(1)}, s32[16]{0:T(128)S(1)}, u32[]{:S(2)}, u32[]{:S(2)}) collective-permute-start(s32[16]{0:T(128)S(1)} %get-tuple-element.17), channel_id=1, source_target_pairs={{4,0},{5,1},{6,2},{7,3},{8,4},{9,5},{10,6},{11,7},{12,8},{13,9},{1... | collective-permute-start | bytes 200 | tf_op jit(solution)/shard_map/ppermute | solution.py:21
  14.8 21.4 %collective-permute-start = (s32[16]{0:T(128)S(1)}, s32[16]{0:T(128)S(1)}, u32[]{:S(2)}, u32[]{:S(2)}) collective-permute-start(s32[16]{0:T(128)S(1)} %get-tuple-element.18), channel_id=1, source_target_pairs={{5,0},{6,1},{7,2},{9,4},{10,5},{11,6},{13,8},{14,9},{15,10},{17,12... | collective-permute-start | bytes 200 | tf_op jit(solution)/shard_map/ppermute | solution.py:21
  18.4 19.8 %collective-permute-start.6 = (s32[16]{0:T(128)S(1)}, s32[16]{0:T(128)S(1)}, u32[]{:S(2)}, u32[]{:S(2)}) collective-permute-start(s32[16]{0:T(128)S(1)} %get-tuple-element.15), channel_id=1, source_target_pairs={{1,0},{2,1},{3,2},{5,4},{6,5},{7,6},{9,8},{10,9},{11,10},{13,12},{... | collective-permute-start | bytes 200 | tf_op jit(solution)/shard_map/ppermute | solution.py:21
  20.3 21.9 %collective-permute-start.4 = (s32[16]{0:T(128)S(1)}, s32[16]{0:T(128)S(1)}, u32[]{:S(2)}, u32[]{:S(2)}) collective-permute-start(s32[16]{0:T(128)S(1)} %get-tuple-element.16), channel_id=1, source_target_pairs={{4,1},{5,2},{6,3},{8,5},{9,6},{10,7},{12,9},{13,10},{14,11},{16,13... | collective-permute-start | bytes 200 | tf_op jit(solution)/shard_map/ppermute | solution.py:21
  23.7 18.5 %collective-permute-start.10 = (s32[16]{0:T(128)S(1)}, s32[16]{0:T(128)S(1)}, u32[]{:S(2)}, u32[]{:S(2)}) collective-permute-start(s32[16]{0:T(128)S(1)} %get-tuple-element.13), channel_id=1, source_target_pairs={{1,4},{2,5},{3,6},{5,8},{6,9},{7,10},{9,12},{10,13},{11,14},{13,16... | collective-permute-start | bytes 200 | tf_op jit(solution)/shard_map/ppermute | solution.py:21
  29.5 2.0 %copy-start.3 = (s32[64,8]{0,1:T(8,128)S(1)}, s32[64,8]{0,1:T(8,128)}, u32[]{:S(2)}) copy-start(s32[64,8]{0,1:T(8,128)} %param.11) | copy-start | bytes 6148
  31.7 14.2 %collective-permute-start.8 = (s32[16]{0:T(128)S(1)}, s32[16]{0:T(128)S(1)}, u32[]{:S(2)}, u32[]{:S(2)}) collective-permute-start(s32[16]{0:T(128)S(1)} %get-tuple-element.14), channel_id=1, source_target_pairs={{0,1},{1,2},{2,3},{4,5},{5,6},{6,7},{8,9},{9,10},{10,11},{12,13},{... | collective-permute-start | bytes 200 | tf_op jit(solution)/shard_map/ppermute | solution.py:21
  36.2 9.7 %collective-permute-start.14 = (s32[16]{0:T(128)S(1)}, s32[16]{0:T(128)S(1)}, u32[]{:S(2)}, u32[]{:S(2)}) collective-permute-start(s32[16]{0:T(128)S(1)} %get-tuple-element.12), channel_id=1, source_target_pairs={{0,5},{1,6},{2,7},{4,9},{5,10},{6,11},{8,13},{9,14},{10,15},{12,17... | collective-permute-start | bytes 200 | tf_op jit(solution)/shard_map/ppermute | solution.py:21
  38.2 7.8 %collective-permute-start.12 = (s32[16]{0:T(128)S(1)}, s32[16]{0:T(128)S(1)}, u32[]{:S(2)}, u32[]{:S(2)}) collective-permute-start(s32[16]{0:T(128)S(1)} %get-tuple-element.19), channel_id=1, source_target_pairs={{0,4},{1,5},{2,6},{3,7},{4,8},{5,9},{6,10},{7,11},{8,12},{9,13},{1... | collective-permute-start | bytes 200 | tf_op jit(solution)/shard_map/ppermute | solution.py:21
  42.3 22.1 %all-to-all-start.1 = ((f32[32,4,6,256]{3,1,2,0:T(4,128)}), f32[32,4,6,256]{3,1,2,0:T(4,128)S(1)}, u32[]{:S(2)}, u32[]{:S(2)}) async-start(f32[32,4,6,256]{3,1,2,0:T(4,128)} %copy_multiply_fusion), calls=%async_computation.1 | async-start | bytes 1572864 | tf_op jit(solution)/shard_map/all_to_all | solution.py:122
  65.7 22.1 %copy-start.1 = (f32[64,6,256]{2,0,1:T(8,128)}, f32[64,6,256]{2,0,1:T(8,128)S(1)}, u32[]{:S(2)}) copy-start(f32[64,6,256]{2,0,1:T(8,128)S(1)} %fusion.3) | copy-start | bytes 1179652
  67.2 21.2 %collective-permute-start.1 = (f32[16,6,256]{2,1,0:T(8,128)}, f32[16,6,256]{2,1,0:T(8,128)}, u32[]{:S(2)}, u32[]{:S(2)}) collective-permute-start(f32[16,6,256]{2,1,0:T(8,128)} %gather_fusion.2), channel_id=1, source_target_pairs={{0,5},{1,6},{2,7},{4,9},{5,10},{6,11},{8,13},{9,14},{10,15},{12,17... | collective-permute-start | bytes 294920 | tf_op jit(solution)/shard_map/ppermute | solution.py:21
  73.1 19.0 %collective-permute-start.3 = (f32[16,6,256]{2,1,0:T(8,128)}, f32[16,6,256]{2,1,0:T(8,128)}, u32[]{:S(2)}, u32[]{:S(2)}) collective-permute-start(f32[16,6,256]{2,1,0:T(8,128)} %gather_fusion.3), channel_id=1, source_target_pairs={{0,4},{1,5},{2,6},{3,7},{4,8},{5,9},{6,10},{7,11},{8,12},{9,13},{1... | collective-permute-start | bytes 294920 | tf_op jit(solution)/shard_map/ppermute | solution.py:21
  76.3 21.0 %collective-permute-start.5 = (f32[16,6,256]{2,1,0:T(8,128)}, f32[16,6,256]{2,1,0:T(8,128)S(1)}, u32[]{:S(2)}, u32[]{:S(2)}) collective-permute-start(f32[16,6,256]{2,1,0:T(8,128)} %gather_fusion.4), channel_id=1, source_target_pairs={{1,4},{2,5},{3,6},{5,8},{6,9},{7,10},{9,12},{10,13},{11,14},{13,16... | collective-permute-start | bytes 294920 | tf_op jit(solution)/shard_map/ppermute | solution.py:21
  80.4 18.9 %collective-permute-start.7 = (f32[16,6,256]{2,1,0:T(8,128)S(1)}, f32[16,6,256]{2,1,0:T(8,128)S(1)}, u32[]{:S(2)}, u32[]{:S(2)}) collective-permute-start(f32[16,6,256]{2,1,0:T(8,128)S(1)} %gather_fusion.5), channel_id=1, source_target_pairs={{0,1},{1,2},{2,3},{4,5},{5,6},{6,7},{8,9},{9,10},{10,11},{12,13},{... | collective-permute-start | bytes 294920 | tf_op jit(solution)/shard_map/ppermute | solution.py:21
  84.7 14.6 %collective-permute-start.9 = (f32[16,6,256]{2,1,0:T(8,128)S(1)}, f32[16,6,256]{2,1,0:T(8,128)S(1)}, u32[]{:S(2)}, u32[]{:S(2)}) collective-permute-start(f32[16,6,256]{2,1,0:T(8,128)S(1)} %gather_fusion.6), channel_id=1, source_target_pairs={{1,0},{2,1},{3,2},{5,4},{6,5},{7,6},{9,8},{10,9},{11,10},{13,12},{... | collective-permute-start | bytes 294920 | tf_op jit(solution)/shard_map/ppermute | solution.py:21
  88.4 10.9 %collective-permute-start.11 = (f32[16,6,256]{2,1,0:T(8,128)S(1)}, f32[16,6,256]{2,1,0:T(8,128)S(1)}, u32[]{:S(2)}, u32[]{:S(2)}) collective-permute-start(f32[16,6,256]{2,1,0:T(8,128)S(1)} %gather_fusion.7), channel_id=1, source_target_pairs={{4,1},{5,2},{6,3},{8,5},{9,6},{10,7},{12,9},{13,10},{14,11},{16,13... | collective-permute-start | bytes 294920 | tf_op jit(solution)/shard_map/ppermute | solution.py:21
  92.1 7.7 %collective-permute-start.13 = (f32[16,6,256]{2,1,0:T(8,128)S(1)}, f32[16,6,256]{2,1,0:T(8,128)S(1)}, u32[]{:S(2)}, u32[]{:S(2)}) collective-permute-start(f32[16,6,256]{2,1,0:T(8,128)S(1)} %gather_fusion.8), channel_id=1, source_target_pairs={{4,0},{5,1},{6,2},{7,3},{8,4},{9,5},{10,6},{11,7},{12,8},{13,9},{1... | collective-permute-start | bytes 294920 | tf_op jit(solution)/shard_map/ppermute | solution.py:21
  97.3 8.1 %collective-permute-start.15 = (f32[16,6,256]{2,1,0:T(8,128)S(1)}, f32[16,6,256]{2,1,0:T(8,128)S(1)}, u32[]{:S(2)}, u32[]{:S(2)}) collective-permute-start(f32[16,6,256]{2,1,0:T(8,128)S(1)} %gather_fusion.9), channel_id=1, source_target_pairs={{5,0},{6,1},{7,2},{9,4},{10,5},{11,6},{13,8},{14,9},{15,10},{17,12... | collective-permute-start | bytes 294920 | tf_op jit(solution)/shard_map/ppermute | solution.py:21

commit v2 on v1

--- a/solution.py
+++ b/solution.py
@@ -11,15 +11,6 @@
 CORE_SQUARED = 0.01
 OFFSET_ROWS = (-1, -1, -1, 0, 0, 1, 1, 1)
 OFFSET_COLS = (-1, 0, 1, -1, 1, -1, 0, 1)
-
-def shifted(values, off_a, off_b, rows_bx, rows_by):
-    pairs = []
-    for a in range(rows_bx):
-        for b in range(rows_by):
-            if 0 <= a + off_a < rows_bx and 0 <= b + off_b < rows_by:
-                pairs.append((a * rows_by + b, (a + off_a) * rows_by + b + off_b))
-    return lax.ppermute(values, ("bx", "by"), pairs)
-
 
 def split3(value):
     first = value.astype(jnp.bfloat16).astype(jnp.float32)
@@ -54,7 +45,7 @@
         moments[index] = jnp.concatenate([high, rows - high], axis=0).astype(jnp.bfloat16)
         return carry
 
-    lax.fori_loop(0, combined.shape[0], prepare, 0)
+    lax.fori_loop(0, combined.shape[0], prepare, 0, unroll=4)
 
     def target(index, carry):
         x = combined[index, 0:3, :] - middle
@@ -94,6 +85,139 @@
     lax.fori_loop(0, own, target, 0)
 
 
+MESH = pl.DeviceIdType.MESH
+
+
+def exchange(rows_bx, rows_by, pair_most, starts, positions, strengths, arrived, outgoing, send_sem, recv_sem):
+    devices = rows_bx * rows_by
+    slots = positions.shape[0]
+    me = lax.axis_index("bx") * rows_by + lax.axis_index("by")
+
+    def place(step):
+        other = lax.rem(me + step, devices)
+        return other, (other // rows_by, lax.rem(other, rows_by))
+
+    barrier = pltpu.get_barrier_semaphore()
+
+    def greet(step, carry):
+        pl.semaphore_signal(barrier, inc=1, device_id=place(step)[1], device_id_type=MESH)
+        return carry
+
+    lax.fori_loop(1, devices, greet, 0)
+
+    def pack(other, target, row):
+        for k in range(pair_most):
+            slot = jnp.minimum(starts[other] + k, slots - 1)
+            target[row, k, 0:3, :] = positions[slot]
+            target[row, k, 3:6, :] = strengths[slot]
+
+    def pack_step(step, carry):
+        pack(place(step)[0], outgoing, step)
+        return carry
+
+    lax.fori_loop(1, devices, pack_step, 0)
+    pack(me, arrived, me)
+    pl.semaphore_wait(barrier, devices - 1)
+
+    def copy(step):
+        return pltpu.make_async_remote_copy(
+            src_ref=outgoing.at[step],
+            dst_ref=arrived.at[me],
+            send_sem=send_sem.at[step],
+            recv_sem=recv_sem.at[step],
+            device_id=place(step)[1],
+            device_id_type=MESH,
+        )
+
+    def start(step, carry):
+        copy(step).start()
+        return carry
+
+    lax.fori_loop(1, devices, start, 0)
+
+    def finish(step, carry):
+        pltpu.make_async_remote_copy(
+            src_ref=outgoing.at[step],
+            dst_ref=arrived.at[lax.rem(me + devices - step, devices)],
+            send_sem=send_sem.at[step],
+            recv_sem=recv_sem.at[step],
+            device_id=place(step)[1],
+            device_id_type=MESH,
+        ).wait()
+        return carry
+
+    lax.fori_loop(1, devices, finish, 0)
+
+
+def ghosts(rows_bx, rows_by, own, picks, count, requests, arrived, combined, served, send_sem, recv_sem):
+    leaf = arrived.shape[2]
+    room = requests.shape[1]
+    row_a = lax.axis_index("bx")
+    row_b = lax.axis_index("by")
+    barrier = pltpu.get_barrier_semaphore()
+
+    def there(direction, sign):
+        a = row_a + sign * OFFSET_ROWS[direction]
+        b = row_b + sign * OFFSET_COLS[direction]
+        return (a, b), (a >= 0) & (a < rows_bx) & (b >= 0) & (b < rows_by)
+
+    for direction in range(8):
+        device, exists = there(direction, 1)
+
+        @pl.when(exists)
+        def _(device=device):
+            pl.semaphore_signal(barrier, inc=1, device_id=device, device_id_type=MESH)
+
+    position = lax.broadcasted_iota(jnp.int32, (6, leaf), 1)
+
+    def owned_leaf(index):
+        return jnp.where(position < count[index], arrived[picks[index]], 0.0)
+
+    tall = 1 + (row_a > 0).astype(jnp.int32) + (row_a < rows_bx - 1).astype(jnp.int32)
+    wide = 1 + (row_b > 0).astype(jnp.int32) + (row_b < rows_by - 1).astype(jnp.int32)
+    pl.semaphore_wait(barrier, tall * wide - 1)
+
+    def copy(direction):
+        return pltpu.make_async_remote_copy(
+            src_ref=served.at[direction],
+            dst_ref=combined.at[pl.ds(own + direction * room, room)],
+            send_sem=send_sem.at[direction],
+            recv_sem=recv_sem.at[direction],
+            device_id=there(direction, -1)[0],
+            device_id_type=MESH,
+        )
+
+    for direction in range(8):
+        _, exists = there(direction, -1)
+
+        @pl.when(exists)
+        def _(direction=direction):
+            def serve(index, carry):
+                served[direction, index] = owned_leaf(requests[direction, index])
+                return carry
+
+            lax.fori_loop(0, room, serve, 0, unroll=4)
+            copy(direction).start()
+
+    def own_leaf(index, carry):
+        combined[index] = owned_leaf(index)
+        return carry
+
+    lax.fori_loop(0, own, own_leaf, 0, unroll=4)
+    for direction in range(8):
+        _, exists = there(direction, -1)
+
+        @pl.when(exists)
+        def _(direction=direction):
+            copy(direction).wait_send()
+
+        _, exists = there(direction, 1)
+
+        @pl.when(exists)
+        def _(direction=direction):
+            copy(direction).wait_recv()
+
+
 def local(positions, strengths, blob_count, split_counts, ghost_ids, near_list):
     rows_bx = lax.axis_size("bx")
     rows_by = lax.axis_size("by")
@@ -102,44 +226,67 @@
     pair_most = slots // devices
     leaf = positions.shape[2]
     own = near_list.shape[0]
-    requests = [
-        shifted(ghost_ids[0, direction], OFFSET_ROWS[direction], OFFSET_COLS[direction], rows_bx, rows_by)
-        for direction in range(8)
-    ]
+    room = ghost_ids.shape[2]
+    row_a = lax.axis_index("bx")
+    row_b = lax.axis_index("by")
+    me = row_a * rows_by + row_b
+    smem = pl.BlockSpec(memory_space=pltpu.SMEM)
+    vmem = pl.BlockSpec(memory_space=pltpu.VMEM)
     counts_row = split_counts[0]
     starts = jnp.cumsum(counts_row) - counts_row
-    within = jnp.arange(pair_most, dtype=jnp.int32)
-    pick = jnp.minimum(starts[:, None] + within[None, :], slots - 1).reshape(-1)
-    valid = (within[None, :] < counts_row[:, None]).reshape(-1)
-    stacked = jnp.concatenate([positions, strengths], axis=1)[pick]
-    sent_count = jnp.where(valid, blob_count[pick], 0)
-    sent_live = (jnp.arange(leaf, dtype=jnp.int32)[None, :] < sent_count[:, None]).astype(
-        jnp.float32
-    )
-    outgoing = (stacked * sent_live[:, None, :]).reshape(devices, pair_most, 6, leaf)
-    out_count = sent_count.astype(jnp.float32).reshape(devices, pair_most)
-    arrived, arrived_count = (
-        lax.all_to_all(outgoing, ("bx", "by"), split_axis=0, concat_axis=0, tiled=True),
-        lax.all_to_all(out_count, ("bx", "by"), split_axis=0, concat_axis=0, tiled=True),
-    )
-    arrived_valid = arrived_count > 0.0
-    per_source = jnp.sum(arrived_valid.astype(jnp.int32), axis=1)
-    prefix = jnp.cumsum(per_source) - per_source
-    placed = jnp.where(arrived_valid, prefix[:, None] + within[None, :], own).reshape(-1)
-    selector = (jnp.arange(own, dtype=jnp.int32)[:, None] == placed[None, :]).astype(jnp.float32)
-    owned_blobs = jnp.dot(
-        selector, arrived.reshape(devices * pair_most, 6 * leaf), precision=lax.Precision.HIGHEST
-    ).reshape(own, 6, leaf)
-    own_count = jnp.dot(selector, arrived_count.reshape(-1), precision=lax.Precision.HIGHEST)
-    ghost_blocks = []
-    for direction in range(8):
-        served = owned_blobs[requests[direction]]
-        ghost_blocks.append(
-            shifted(served, -OFFSET_ROWS[direction], -OFFSET_COLS[direction], rows_bx, rows_by)
-        )
-    combined = jnp.concatenate([owned_blobs] + ghost_blocks, axis=0)
-    smem = pl.BlockSpec(memory_space=pltpu.SMEM)
-    vmem = pl.BlockSpec(memory_space=pltpu.VMEM)
+    facts = jnp.concatenate([ghost_ids.reshape(-1), counts_row, blob_count])
+    table = lax.all_gather(facts, ("bx", "by"), axis=0, tiled=False)
+    arrived = pl.pallas_call(
+        functools.partial(exchange, rows_bx, rows_by, pair_most),
+        out_shape=jax.ShapeDtypeStruct((devices, pair_most, 6, leaf), jnp.float32),
+        in_specs=[smem, vmem, vmem],
+        out_specs=vmem,
+        scratch_shapes=[
+            pltpu.VMEM((devices, pair_most, 6, leaf), jnp.float32),
+            pltpu.SemaphoreType.DMA((devices,)),
+            pltpu.SemaphoreType.DMA((devices,)),
+        ],
+        compiler_params=pltpu.CompilerParams(
+            collective_id=0, has_side_effects=True, vmem_limit_bytes=32 * 1024 * 1024
+        ),
+        name="exchange",
+    )(starts, positions, strengths)
+    asked = table[:, : 8 * room].reshape(devices, 8, room)
+    every = table[:, 8 * room : 8 * room + devices]
+    slot_count = table[:, 8 * room + devices :]
+    reader = jnp.stack(
+        [me - OFFSET_ROWS[q] * rows_by - OFFSET_COLS[q] for q in range(8)]
+    )
+    device_ids = jnp.arange(devices, dtype=jnp.int32)
+    requests = jnp.sum(
+        jnp.where(device_ids[:, None, None] == reader[None, :, None], asked, 0), axis=0
+    )
+    to_me = jnp.sum(jnp.where(device_ids[None, :] == me, every, 0), axis=1)
+    start_of = jnp.sum(jnp.where(device_ids[None, :] < me, every, 0), axis=1)
+    earlier = device_ids[:, None] < device_ids[None, :]
+    prefix = jnp.sum(jnp.where(earlier, to_me[:, None], 0), axis=0)
+    rank = jnp.arange(own, dtype=jnp.int32)[:, None] - prefix[None, :]
+    mine = (rank >= 0) & (rank < to_me[None, :])
+    picks = jnp.sum(jnp.where(mine, device_ids[None, :] * pair_most + rank, 0), axis=1)
+    wanted = jnp.sum(
+        jnp.where(mine, device_ids[None, :] * slots + start_of[None, :] + rank, 0), axis=1
+    )
+    own_count = slot_count.reshape(-1)[wanted]
+    combined = pl.pallas_call(
+        functools.partial(ghosts, rows_bx, rows_by, own),
+        out_shape=jax.ShapeDtypeStruct((own + 8 * room, 6, leaf), jnp.float32),
+        in_specs=[smem, smem, smem, vmem],
+        out_specs=vmem,
+        scratch_shapes=[
+            pltpu.VMEM((8, room, 6, leaf), jnp.float32),
+            pltpu.SemaphoreType.DMA((8,)),
+            pltpu.SemaphoreType.DMA((8,)),
+        ],
+        compiler_params=pltpu.CompilerParams(
+            collective_id=1, has_side_effects=True, vmem_limit_bytes=32 * 1024 * 1024
+        ),
+        name="ghosts",
+    )(picks, own_count, requests, arrived.reshape(devices * pair_most, 6, leaf))
     velocity = pl.pallas_call(
         functools.partial(near_field, own),
         out_shape=jax.ShapeDtypeStruct((own, 3, leaf), jnp.float32),
@@ -151,8 +298,8 @@
         ],
         compiler_params=pltpu.CompilerParams(vmem_limit_bytes=48 * 1024 * 1024),
         name="near_field",
-    )(near_list, own_count.astype(jnp.int32), combined)
-    return (owned_blobs, velocity)
+    )(near_list, own_count, combined)
+    return (combined[:own], velocity)
 
 
 def solution(mesh):

time: 204 us -> 170 us (0.83)
  starting transfers between devices: 59.3 us -> 0 us
  blocking collectives: 0 us -> 39.8 us
  Pallas kernels: 97.1 us -> 122 us
  waiting for transfers between devices: 21.9 us -> 0 us
  local copies, waits for them, and re-layouts: 17.5 us -> 5.24 us
  other arithmetic: 5.55 us -> 1.52 us
    pallas_call x0 -> x2, Pallas kernels: none -> 49.4 us  [the longest x1 30.9 us: local(): pl.pallas_call(functools.partial(exchange, rows_bx, rows_by, pair_most),...]
    ppermute x16 -> x0, starting transfers between devices: 49.3 us -> none  [shifted(): return lax.ppermute(values, ('bx', 'by'), pairs)]
    unnamed x0 -> x1, blocking collectives: none -> 39.8 us
    pallas_call x1, Pallas kernels: 97.1 us -> 72.6 us  [local(): pl.pallas_call(functools.partial(near_field, own), out_shape=jax.ShapeDty...]
    all_to_all x2 -> x0, waiting for transfers between devices: 15.8 us -> none  [the longest x1 15.8 us: local(): lax.all_to_all(outgoing, ('bx', 'by'), split_axis=0, concat_axis=0, tiled...]
    all_to_all x2 -> x0, starting transfers between devices: 9.95 us -> none  [the longest x1 6.33 us: local(): lax.all_to_all(out_count, ('bx', 'by'), split_axis=0, concat_axis=0, tile...]
    gather x13 -> x1, local copies, waits for them, and re-layouts: 8.76 us -> 0.77 us  [local(): own_count = slot_count.reshape(-1)[wanted]]
    ppermute x16 -> x0, waiting for transfers between devices: 6.07 us -> none  [shifted(): return lax.ppermute(values, ('bx', 'by'), pairs)]
  transfers between devices with their start and end apart: 18 -> 0, of which waited for: 3 -> 0; matrix products, arithmetic and copies ran while one was open for 8% -> 0% of each run, Pallas kernels for 0% -> 0%
where the time goes in v2:
time: 170 us; the launch traced here: 169 us
  Pallas kernels  122 us (72%)
  blocking collectives  39.8 us (23%)
  local copies, waits for them, and re-layouts  5.24 us (3%)
    pallas_call x1, Pallas kernels, local(): pl.pallas_call(functools.partial(near_field, own), out_shape=jax.ShapeDty...  72.6 us
    unnamed x1, blocking collectives  39.8 us
    pallas_call x1, Pallas kernels, local(): pl.pallas_call(functools.partial(exchange, rows_bx, rows_by, pair_most),...  30.9 us
    pallas_call x1, Pallas kernels, local(): pl.pallas_call(functools.partial(ghosts, rows_bx, rows_by, own), out_shap...  18.5 us

profile of v2, /device:TPU:11, one launch (start us, length us, event | category | flops | bytes accessed | tf_op | source)
XLA Modules:
  0.0 169.3 jit_solution(12383680520647490571)
XLA Ops:
  0.6 0.0 copy-start.2
  0.6 0.0 copy-start
  0.7 0.1 stack.35
  0.8 0.1 iota_compare_fusion.1
  0.8 0.1 copy.27
  0.9 0.8 reshape.105
  1.7 0.9 add_dynamic-update-slice_fusion
  2.6 39.8 %all-reduce = s32[9216]{0:T(1024)S(1)} all-reduce(s32[9216]{0:T(1024)S(1)} %add_dynamic-update-slice_fusion), channel_id=2, replica_groups=mesh['bx'=8,'by'=4] {'bx','by'}, use_global_device_ids=true, to_apply=%add | all-reduce | flops 9216 | bytes 73728
  42.4 0.1 reshape.118
  42.5 0.1 fusion
  42.6 0.1 select_reduce_fusion.1
  42.7 0.1 select_reduce_fusion.3
  42.8 0.1 select_reduce_fusion
  42.9 0.8 gather_fusion
  43.7 0.1 reduce_sum.65.requests
  43.8 1.3 copy.29.positions
  45.0 0.0 copy-done
  45.1 0.3 copy.30.strengths
  45.3 0.0 copy-done.2
  45.3 0.1 copy.28
  45.4 0.1 reduce-window.9
  45.5 0.1 reduce.1
  45.6 30.9 %exchange.1 = f32[32,4,6,256]{3,2,1,0:T(8,128)S(1)} custom-call(s32[32]{0:T(128)S(1)} %bitcast_subtract_fusion.starts, f32[128,3,256]{2,1,0:T(4,128)S(1)} %copy.29.positions, f32[128,3,256]{2,1,0:T(4,128)S(1)} %copy.30.strengths), custom_call_target="tpu_custom_call" | custom-call | tf_op jit(solution)/shard_map/exchange/pallas_call | solution.py:239
  76.5 18.5 %ghosts.1.combined = f32[192,6,256]{2,1,0:T(8,128)S(1)} custom-call(s32[64]{0:T(128)S(1)} %get-tuple-element.13.picks, s32[64]{0:T(128)S(1)} %gather_fusion, s32[8,16]{1,0:T(8,128)S(1)} %reduce_sum.65.requests, f32[128,6,256]{2,1,0:T(8,128)S(1)} %bitcast.19), custom_call_target="tpu_custom_call" | custom-call | tf_op jit(solution)/shard_map/ghosts/pallas_call | solution.py:275
  95.0 0.0 copy-start.1
  95.1 0.9 copy.32
  95.9 0.0 copy-done.1
  95.9 0.1 copy.31.near
  96.0 72.6 %near_field.1 = f32[64,3,256]{2,1,0:T(4,128)S(1)} custom-call(s32[64,8]{1,0:T(8,128)S(1)} %copy.31.near, s32[64]{0:T(128)S(1)} %gather_fusion, f32[192,6,256]{2,1,0:T(8,128)S(1)} %ghosts.1.combined), custom_call_target="tpu_custom_call" | custom-call | tf_op jit(solution)/shard_map/near_field/pallas_call | solution.py:290
  168.6 0.7 copy.33
  (9 shorter events, 0.1 us)
Async XLA Ops:
  0.6 44.7 %copy-start.2 = (s32[1,32]{1,0:T(1,128)S(1)}, s32[1,32]{1,0:T(1,128)}, u32[]{:S(2)}) copy-start(s32[1,32]{1,0:T(1,128)} %param.9) | copy-start | bytes 388
  0.6 44.4 %copy-start = (f32[128,3,256]{2,0,1:T(8,128)S(1)}, f32[128,3,256]{2,0,1:T(8,128)}, u32[]{:S(2)}) copy-start(f32[128,3,256]{2,0,1:T(8,128)} %param.7) | copy-start | bytes 1179652
  95.0 0.9 copy-start.1

commit v3 on v2

--- a/solution.py
+++ b/solution.py
@@ -88,7 +88,7 @@
 MESH = pl.DeviceIdType.MESH
 
 
-def exchange(rows_bx, rows_by, pair_most, starts, positions, strengths, arrived, outgoing, send_sem, recv_sem):
+def exchange(rows_bx, rows_by, pair_most, starts, facts, positions, strengths, arrived, table, outgoing, send_sem, recv_sem, fact_send, fact_recv):
     devices = rows_bx * rows_by
     slots = positions.shape[0]
     me = lax.axis_index("bx") * rows_by + lax.axis_index("by")
@@ -110,6 +110,16 @@
             slot = jnp.minimum(starts[other] + k, slots - 1)
             target[row, k, 0:3, :] = positions[slot]
             target[row, k, 3:6, :] = strengths[slot]
+
+    def fact_copy(step, writer):
+        return pltpu.make_async_remote_copy(
+            src_ref=facts,
+            dst_ref=table.at[writer],
+            send_sem=fact_send.at[step],
+            recv_sem=fact_recv.at[step],
+            device_id=place(step)[1],
+            device_id_type=MESH,
+        )
 
     def pack_step(step, carry):
         pack(place(step)[0], outgoing, step)
@@ -130,10 +140,12 @@
         )
 
     def start(step, carry):
+        fact_copy(step, me).start()
         copy(step).start()
         return carry
 
     lax.fori_loop(1, devices, start, 0)
+    table[me] = facts[...]
 
     def finish(step, carry):
         pltpu.make_async_remote_copy(
@@ -144,6 +156,7 @@
             device_id=place(step)[1],
             device_id_type=MESH,
         ).wait()
+        fact_copy(step, lax.rem(me + devices - step, devices)).wait()
         return carry
 
     lax.fori_loop(1, devices, finish, 0)
@@ -235,14 +248,20 @@
     counts_row = split_counts[0]
     starts = jnp.cumsum(counts_row) - counts_row
     facts = jnp.concatenate([ghost_ids.reshape(-1), counts_row, blob_count])
-    table = lax.all_gather(facts, ("bx", "by"), axis=0, tiled=False)
-    arrived = pl.pallas_call(
+    lines = -(-facts.shape[0] // 128)
+    facts = jnp.pad(facts, (0, lines * 128 - facts.shape[0])).reshape(lines, 128)
+    arrived, table = pl.pallas_call(
         functools.partial(exchange, rows_bx, rows_by, pair_most),
-        out_shape=jax.ShapeDtypeStruct((devices, pair_most, 6, leaf), jnp.float32),
-        in_specs=[smem, vmem, vmem],
-        out_specs=vmem,
+        out_shape=(
+            jax.ShapeDtypeStruct((devices, pair_most, 6, leaf), jnp.float32),
+            jax.ShapeDtypeStruct((devices, lines, 128), jnp.int32),
+        ),
+        in_specs=[smem, vmem, vmem, vmem],
+        out_specs=(vmem, vmem),
         scratch_shapes=[
             pltpu.VMEM((devices, pair_most, 6, leaf), jnp.float32),
+            pltpu.SemaphoreType.DMA((devices,)),
+            pltpu.SemaphoreType.DMA((devices,)),
             pltpu.SemaphoreType.DMA((devices,)),
             pltpu.SemaphoreType.DMA((devices,)),
         ],
@@ -250,10 +269,11 @@
             collective_id=0, has_side_effects=True, vmem_limit_bytes=32 * 1024 * 1024
         ),
         name="exchange",
-    )(starts, positions, strengths)
+    )(starts, facts, positions, strengths)
+    table = table.reshape(devices, lines * 128)
     asked = table[:, : 8 * room].reshape(devices, 8, room)
     every = table[:, 8 * room : 8 * room + devices]
-    slot_count = table[:, 8 * room + devices :]
+    slot_count = table[:, 8 * room + devices : 8 * room + devices + slots]
     reader = jnp.stack(
         [me - OFFSET_ROWS[q] * rows_by - OFFSET_COLS[q] for q in range(8)]
     )

time: 170 us -> 130 us (0.76)
  blocking collectives: 39.8 us -> 0 us
    unnamed x1 -> x0, blocking collectives: 39.8 us -> none
    unnamed x12 -> x14, local copies, waits for them, and re-layouts: 3.23 us -> 4.24 us
where the time goes in v3:
time: 130 us
  Pallas kernels  123 us (95%)
  local copies, waits for them, and re-layouts  5.47 us (4%)
    pallas_call x1, Pallas kernels, local(): pl.pallas_call(functools.partial(near_field, own), out_shape=jax.ShapeDty...  72.6 us
    pallas_call x1, Pallas kernels, local(): pl.pallas_call(functools.partial(exchange, rows_bx, rows_by, pair_most),...  31.2 us
    pallas_call x1, Pallas kernels, local(): pl.pallas_call(functools.partial(ghosts, rows_bx, rows_by, own), out_shap...  19.5 us
    unnamed x14, local copies, waits for them, and re-layouts  4.24 us

profile of v3, /device:TPU:11, one launch (start us, length us, event | category | flops | bytes accessed | tf_op | source)
XLA Modules:
  0.0 130.3 jit_solution(10173367245375902932)
XLA Ops:
  0.6 0.0 copy-start.2
  0.6 0.0 copy-start.1
  0.7 0.0 copy-start.3
  0.7 0.1 stack.35
  0.8 0.1 iota_compare_fusion.1
  0.9 0.1 copy.24
  0.9 1.3 copy.22.positions
  2.2 1.3 copy.23.strengths
  3.5 0.0 copy-done.2
  3.5 0.1 copy.21
  3.6 0.1 reduce-window.9
  3.6 0.1 reduce.1
  3.8 0.0 copy-done.1
  3.8 0.1 reshape.113
  3.9 0.0 copy-done.3
  3.9 0.1 pad_add_fusion
  3.9 31.2 %exchange.1 = (f32[32,4,6,256]{3,2,1,0:T(8,128)S(1)}, s32[32,3,128]{2,1,0:T(4,128)S(1)}) custom-call(s32[32]{0:T(128)S(1)} %bitcast_subtract_fusion.starts, s32[3,128]{1,0:T(4,128)S(1)} %pad_bitcast_fusion.facts, f32[128,3,256]{2,1,0:T(4,128)S(1)} %copy.22.positions, f32[128,3,256]{2,1,0:T(4,128)S(1)} %copy.23.strengths), custom_call_target="tpu_custom_call" | custom-call | tf_op jit(solution)/shard_map/exchange/pallas_call | solution.py:253
  35.2 0.1 fusion
  35.2 0.1 select_reduce_fusion.1
  35.4 0.1 select_reduce_fusion.3
  35.5 0.1 select_reduce_fusion
  35.6 0.0 copy-start
  35.6 0.8 gather_fusion
  36.4 0.1 reduce_sum.65.requests
  36.5 19.5 %ghosts.1.combined = f32[192,6,256]{2,1,0:T(8,128)S(1)} custom-call(s32[64]{0:T(128)S(1)} %get-tuple-element.15.picks, s32[64]{0:T(128)S(1)} %gather_fusion, s32[8,16]{1,0:T(8,128)S(1)} %reduce_sum.65.requests, f32[128,6,256]{2,1,0:T(8,128)S(1)} %bitcast.25), custom_call_target="tpu_custom_call" | custom-call | tf_op jit(solution)/shard_map/ghosts/pallas_call | solution.py:295
  56.0 0.0 copy-done
  56.0 0.1 copy.25.near
  56.1 72.6 %near_field.1 = f32[64,3,256]{2,1,0:T(4,128)S(1)} custom-call(s32[64,8]{1,0:T(8,128)S(1)} %copy.25.near, s32[64]{0:T(128)S(1)} %gather_fusion, f32[192,6,256]{2,1,0:T(8,128)S(1)} %ghosts.1.combined), custom_call_target="tpu_custom_call" | custom-call | tf_op jit(solution)/shard_map/near_field/pallas_call | solution.py:310
  128.7 0.7 copy.27
  129.4 0.9 copy.26
  (10 shorter events, 0.1 us)
Async XLA Ops:
  0.6 2.9 %copy-start.2 = (s32[1,32]{1,0:T(1,128)S(1)}, s32[1,32]{1,0:T(1,128)}, u32[]{:S(2)}) copy-start(s32[1,32]{1,0:T(1,128)} %param.9) | copy-start | bytes 388
  0.6 3.1 %copy-start.1 = (s32[1,8,16]{2,1,0:T(8,128)S(1)}, s32[1,8,16]{2,1,0:T(8,128)}, u32[]{:S(2)}) copy-start(s32[1,8,16]{2,1,0:T(8,128)} %param.10) | copy-start | bytes 1540
  0.7 3.2 %copy-start.3 = (s32[128]{0:T(128)S(1)}, s32[128]{0:T(128)}, u32[]{:S(2)}) copy-start(s32[128]{0:T(128)} %param.8) | copy-start | bytes 1540
  35.6 20.4 %copy-start = (s32[64,8]{0,1:T(8,128)S(1)}, s32[64,8]{0,1:T(8,128)}, u32[]{:S(2)}) copy-start(s32[64,8]{0,1:T(8,128)} %param.11) | copy-start | bytes 6148

commit v4 on v3

--- a/solution.py
+++ b/solution.py
@@ -82,7 +82,7 @@
         velocity[index] = jnp.where(live, speed * (0.25 / math.pi), 0.0)
         return carry
 
-    lax.fori_loop(0, own, target, 0)
+    lax.fori_loop(0, own, target, 0, unroll=8)
 
 
 MESH = pl.DeviceIdType.MESH

time: 130 us -> 110 us (0.85)
  Pallas kernels: 123 us -> 102 us
    pallas_call x1, Pallas kernels: 72.6 us -> 51.7 us  [local(): pl.pallas_call(functools.partial(near_field, own), out_shape=jax.ShapeDty...]
where the time goes in v4:
time: 110 us; the launch traced here: 109 us
  Pallas kernels  102 us (93%)
  local copies, waits for them, and re-layouts  5.47 us (5%)
    pallas_call x1, Pallas kernels, local(): pl.pallas_call(functools.partial(near_field, own), out_shape=jax.ShapeDty...  51.7 us
    pallas_call x1, Pallas kernels, local(): pl.pallas_call(functools.partial(exchange, rows_bx, rows_by, pair_most),...  31.2 us
    pallas_call x1, Pallas kernels, local(): pl.pallas_call(functools.partial(ghosts, rows_bx, rows_by, own), out_shap...  19.5 us
    unnamed x14, local copies, waits for them, and re-layouts  4.24 us

profile of v4, /device:TPU:11, one launch (start us, length us, event | category | flops | bytes accessed | tf_op | source)
XLA Modules:
  0.0 109.5 jit_solution(17398105355058157550)
XLA Ops:
  0.6 0.0 copy-start.2
  0.6 0.0 copy-start.1
  0.7 0.0 copy-start.3
  0.7 0.1 stack.35
  0.8 0.1 iota_compare_fusion.1
  0.9 0.1 copy.24
  0.9 1.3 %copy.22.positions = f32[128,3,256]{2,1,0:T(4,128)S(1)} copy(f32[128,3,256]{2,0,1:T(8,128)} %param.6) | data formatting | bytes 786432 | tf_op args[0]
  2.2 1.3 %copy.23.strengths = f32[128,3,256]{2,1,0:T(4,128)S(1)} copy(f32[128,3,256]{2,0,1:T(8,128)} %param.7) | data formatting | bytes 786432 | tf_op args[1]
  3.5 0.0 copy-done.2
  3.5 0.1 copy.21
  3.6 0.1 reduce-window.9
  3.6 0.1 reduce.1
  3.8 0.0 copy-done.1
  3.8 0.1 reshape.113
  3.9 0.0 copy-done.3
  3.9 0.1 pad_add_fusion
  3.9 31.2 %exchange.1 = (f32[32,4,6,256]{3,2,1,0:T(8,128)S(1)}, s32[32,3,128]{2,1,0:T(4,128)S(1)}) custom-call(s32[32]{0:T(128)S(1)} %bitcast_subtract_fusion.starts, s32[3,128]{1,0:T(4,128)S(1)} %pad_bitcast_fusion.facts, f32[128,3,256]{2,1,0:T(4,128)S(1)} %copy.22.positions, f32[128,3,256]{2,1,0:T(4,128)S(1)} %copy.23.strengths), custom_call_target="tpu_custom_call" | custom-call | tf_op jit(solution)/shard_map/exchange/pallas_call | solution.py:253
  35.2 0.1 fusion
  35.2 0.1 select_reduce_fusion.1
  35.4 0.1 select_reduce_fusion.3
  35.5 0.1 select_reduce_fusion
  35.6 0.0 copy-start
  35.6 0.8 gather_fusion
  36.4 0.1 reduce_sum.65.requests
  36.5 19.5 %ghosts.1.combined = f32[192,6,256]{2,1,0:T(8,128)S(1)} custom-call(s32[64]{0:T(128)S(1)} %get-tuple-element.15.picks, s32[64]{0:T(128)S(1)} %gather_fusion, s32[8,16]{1,0:T(8,128)S(1)} %reduce_sum.65.requests, f32[128,6,256]{2,1,0:T(8,128)S(1)} %bitcast.25), custom_call_target="tpu_custom_call" | custom-call | tf_op jit(solution)/shard_map/ghosts/pallas_call | solution.py:295
  56.0 0.0 copy-done
  56.0 0.1 copy.25.near
  56.1 51.7 %near_field.1 = f32[64,3,256]{2,1,0:T(4,128)S(1)} custom-call(s32[64,8]{1,0:T(8,128)S(1)} %copy.25.near, s32[64]{0:T(128)S(1)} %gather_fusion, f32[192,6,256]{2,1,0:T(8,128)S(1)} %ghosts.1.combined), custom_call_target="tpu_custom_call" | custom-call | tf_op jit(solution)/shard_map/near_field/pallas_call | solution.py:310
  107.8 0.7 copy.27
  108.6 0.9 copy.26
  (10 shorter events, 0.1 us)
Async XLA Ops:
  0.6 2.9 %copy-start.2 = (s32[1,32]{1,0:T(1,128)S(1)}, s32[1,32]{1,0:T(1,128)}, u32[]{:S(2)}) copy-start(s32[1,32]{1,0:T(1,128)} %param.9) | copy-start | bytes 388
  0.6 3.1 %copy-start.1 = (s32[1,8,16]{2,1,0:T(8,128)S(1)}, s32[1,8,16]{2,1,0:T(8,128)}, u32[]{:S(2)}) copy-start(s32[1,8,16]{2,1,0:T(8,128)} %param.10) | copy-start | bytes 1540
  0.7 3.2 %copy-start.3 = (s32[128]{0:T(128)S(1)}, s32[128]{0:T(128)}, u32[]{:S(2)}) copy-start(s32[128]{0:T(128)} %param.8) | copy-start | bytes 1540
  35.6 20.4 %copy-start = (s32[64,8]{0,1:T(8,128)S(1)}, s32[64,8]{0,1:T(8,128)}, u32[]{:S(2)}) copy-start(s32[64,8]{0,1:T(8,128)} %param.11) | copy-start | bytes 6148

commit v5 on v4

--- a/solution.py
+++ b/solution.py
@@ -121,12 +121,6 @@
             device_id_type=MESH,
         )
 
-    def pack_step(step, carry):
-        pack(place(step)[0], outgoing, step)
-        return carry
-
-    lax.fori_loop(1, devices, pack_step, 0)
-    pack(me, arrived, me)
     pl.semaphore_wait(barrier, devices - 1)
 
     def copy(step):
@@ -140,12 +134,14 @@
         )
 
     def start(step, carry):
+        pack(place(step)[0], outgoing, step)
+        copy(step).start()
         fact_copy(step, me).start()
-        copy(step).start()
         return carry
 
     lax.fori_loop(1, devices, start, 0)
     table[me] = facts[...]
+    pack(me, arrived, me)
 
     def finish(step, carry):
         pltpu.make_async_remote_copy(

time: 110 us -> 110 us (level)
  no operation moved by 1% of the time
where the time goes in v5:
time: 110 us
  Pallas kernels  103 us (94%)
  local copies, waits for them, and re-layouts  5.47 us (5%)
    pallas_call x1, Pallas kernels, local(): pl.pallas_call(functools.partial(near_field, own), out_shape=jax.ShapeDty...  51.7 us
    pallas_call x1, Pallas kernels, local(): pl.pallas_call(functools.partial(exchange, rows_bx, rows_by, pair_most),...  31.4 us
    pallas_call x1, Pallas kernels, local(): pl.pallas_call(functools.partial(ghosts, rows_bx, rows_by, own), out_shap...  19.7 us
    unnamed x14, local copies, waits for them, and re-layouts  4.24 us

profile of v5, /device:TPU:11, one launch (start us, length us, event | category | flops | bytes accessed | tf_op | source)
XLA Modules:
  0.0 109.8 jit_solution(17292812160602606910)
XLA Ops:
  0.6 0.0 copy-start.2
  0.6 0.0 copy-start.1
  0.7 0.0 copy-start.3
  0.7 0.1 stack.35
  0.8 0.1 iota_compare_fusion.1
  0.9 0.1 copy.24
  0.9 1.3 %copy.22.positions = f32[128,3,256]{2,1,0:T(4,128)S(1)} copy(f32[128,3,256]{2,0,1:T(8,128)} %param.6) | data formatting | bytes 786432 | tf_op args[0]
  2.2 1.3 %copy.23.strengths = f32[128,3,256]{2,1,0:T(4,128)S(1)} copy(f32[128,3,256]{2,0,1:T(8,128)} %param.7) | data formatting | bytes 786432 | tf_op args[1]
  3.5 0.0 copy-done.2
  3.5 0.1 copy.21
  3.6 0.1 reduce-window.9
  3.6 0.1 reduce.1
  3.8 0.0 copy-done.1
  3.8 0.1 reshape.113
  3.9 0.0 copy-done.3
  3.9 0.1 pad_add_fusion
  3.9 31.4 %exchange.1 = (f32[32,4,6,256]{3,2,1,0:T(8,128)S(1)}, s32[32,3,128]{2,1,0:T(4,128)S(1)}) custom-call(s32[32]{0:T(128)S(1)} %bitcast_subtract_fusion.starts, s32[3,128]{1,0:T(4,128)S(1)} %pad_bitcast_fusion.facts, f32[128,3,256]{2,1,0:T(4,128)S(1)} %copy.22.positions, f32[128,3,256]{2,1,0:T(4,128)S(1)} %copy.23.strengths), custom_call_target="tpu_custom_call" | custom-call | tf_op jit(solution)/shard_map/exchange/pallas_call | solution.py:249
  35.4 0.1 fusion
  35.5 0.1 select_reduce_fusion.1
  35.6 0.1 select_reduce_fusion.3
  35.7 0.1 select_reduce_fusion
  35.8 0.0 copy-start
  35.8 0.8 gather_fusion
  36.6 0.1 reduce_sum.65.requests
  36.7 19.7 %ghosts.1.combined = f32[192,6,256]{2,1,0:T(8,128)S(1)} custom-call(s32[64]{0:T(128)S(1)} %get-tuple-element.15.picks, s32[64]{0:T(128)S(1)} %gather_fusion, s32[8,16]{1,0:T(8,128)S(1)} %reduce_sum.65.requests, f32[128,6,256]{2,1,0:T(8,128)S(1)} %bitcast.25), custom_call_target="tpu_custom_call" | custom-call | tf_op jit(solution)/shard_map/ghosts/pallas_call | solution.py:291
  56.4 0.0 copy-done
  56.4 0.1 copy.25.near
  56.5 51.7 %near_field.1 = f32[64,3,256]{2,1,0:T(4,128)S(1)} custom-call(s32[64,8]{1,0:T(8,128)S(1)} %copy.25.near, s32[64]{0:T(128)S(1)} %gather_fusion, f32[192,6,256]{2,1,0:T(8,128)S(1)} %ghosts.1.combined), custom_call_target="tpu_custom_call" | custom-call | tf_op jit(solution)/shard_map/near_field/pallas_call | solution.py:306
  108.2 0.7 copy.27
  109.0 0.9 copy.26
  (10 shorter events, 0.1 us)
Async XLA Ops:
  0.6 2.9 %copy-start.2 = (s32[1,32]{1,0:T(1,128)S(1)}, s32[1,32]{1,0:T(1,128)}, u32[]{:S(2)}) copy-start(s32[1,32]{1,0:T(1,128)} %param.9) | copy-start | bytes 388
  0.6 3.1 %copy-start.1 = (s32[1,8,16]{2,1,0:T(8,128)S(1)}, s32[1,8,16]{2,1,0:T(8,128)}, u32[]{:S(2)}) copy-start(s32[1,8,16]{2,1,0:T(8,128)} %param.10) | copy-start | bytes 1540
  0.7 3.2 %copy-start.3 = (s32[128]{0:T(128)S(1)}, s32[128]{0:T(128)}, u32[]{:S(2)}) copy-start(s32[128]{0:T(128)} %param.8) | copy-start | bytes 1540
  35.8 20.5 %copy-start = (s32[64,8]{0,1:T(8,128)S(1)}, s32[64,8]{0,1:T(8,128)}, u32[]{:S(2)}) copy-start(s32[64,8]{0,1:T(8,128)} %param.11) | copy-start | bytes 6148
